TPU v7x, 128 devices: a whole 4x4x4 slice. The times are simulated.
128 devices in a mesh: fsdp: 8 (over z_hi, x), tensor: 16 (over y, z_lo, core).
Axes of the slice: x: 4, y: 4, z: 4 (z_hi: 2, z_lo: 2; z = z_hi * 2 + z_lo), core: 2. Of those that a mesh axis runs over, the one named last changes fastest.
Arguments:
- iterate: bfloat16 [12800, 5120], P('fsdp', 'tensor'), may hold values from -0.0390625 to 0.0390625
Outputs:
- update: bfloat16 [12800, 5120], P('fsdp', 'tensor')
All inputs are finite; a program needn't handle non-finite values.
Results may differ from a plain program's by a relative error of at most 0.0078.
Values may be sent and summed in bfloat16 or wider, within the bound.
A program may use at most 64 MiB of HBM per device.

v0:
```python
import jax
import jax.numpy as jnp
from jax import lax
from jax.sharding import PartitionSpec as P

ROWS = 12800


def transposed_product(left, right):
    return lax.dot_general(
        left, right, (((0,), (0,)), ((), ())), preferred_element_type=jnp.float32
    )


def shards(iterate):
    gathered = lax.all_gather(iterate, "tensor", axis=1, tiled=True)
    partial_value = transposed_product(gathered, iterate)
    summed = lax.psum(partial_value, "fsdp")
    gram_panel = summed.astype(jnp.bfloat16)
    first_product = jnp.dot(gathered, gram_panel, preferred_element_type=jnp.float32).astype(
        jnp.bfloat16
    )
    second_product = jnp.dot(
        lax.all_gather(first_product, "tensor", axis=1, tiled=True),
        gram_panel,
        preferred_element_type=jnp.float32,
    )
    factor = 0.2 * ROWS**0.5
    combined = (
        3.4445 * iterate.astype(jnp.float32)
        - 4.775 * first_product.astype(jnp.float32)
        + 2.0315 * second_product
    )
    return (factor * combined).astype(jnp.bfloat16)


def solution(mesh):
    placed = (P("fsdp", "tensor"),)
    return jax.shard_map(
        shards, mesh=mesh, in_specs=placed, out_specs=P("fsdp", "tensor"), check_vma=False
    )
```

profile of v0, /device:TPU:1, one launch (start us, length us, event | category | flops | bytes accessed | tf_op | source)
XLA Modules:
  0.0 376.2 jit_solution(5191386516596483482)
XLA Ops:
  6.5 0.0 all-gather.3.cloned.1.call-start
  6.5 0.7 all-gather.3.cloned.1.call-update
  7.3 0.0 all-gather.5.cloned.1.call-start
  7.3 98.3 %all-gather.3.cloned.1.call-done = bf16[1600,5120]{0,1:T(8,128)(2,1)} async-done(((bf16[1600,320]{0,1:T(8,128)(2,1)}), bf16[1600,5120]{0,1:T(8,128)(2,1)}) %all-gather.3.cloned.1.call-update) | async-done | bytes 16384016 | tf_op jit(solution)/shard_map/all_gather | solution.py:16
  105.6 11.7 %fusion.6 = f32[5120,320]{0,1:T(8,128)} fusion(bf16[1600,5120]{0,1:T(8,128)(2,1)} %all-gather.3.cloned.1.call-done, bf16[1600,320]{0,1:T(8,128)(2,1)} %param.1), kind=kOutput, calls=%fused_computation.8 | convolution fusion | flops 5242880000 | bytes 23961600 | tf_op jit(solution)/shard_map/dot_general | solution.py:10
  117.3 138.1 %all-reduce.1 = bf16[5120,320]{0,1:T(8,128)(2,1)S(1)} all-reduce(f32[5120,320]{0,1:T(8,128)} %fusion.6), channel_id=1, replica_groups=mesh['fsdp'=8,'tensor'=16] {'fsdp'}, use_global_device_ids=true, to_apply=%region_0.0 | all-reduce | flops 1638400 | bytes 9830400 | tf_op jit(solution)/shard_map/psum | solution.py:18
  255.4 10.8 %fusion.3 = bf16[1600,320]{0,1:T(8,128)(2,1)} fusion(bf16[1600,5120]{0,1:T(8,128)(2,1)} %all-gather.3.cloned.1.call-done, bf16[5120,320]{0,1:T(8,128)(2,1)S(1)} %all-reduce.1), kind=kOutput, calls=%fused_computation.5 | convolution fusion | flops 5243392000 | bytes 20684800 | tf_op jit(solution)/shard_map/dot_general | solution.py:20
  266.2 0.0 all-gather.5.cloned.1.call-update
  266.2 91.3 %all-gather.5.cloned.1.call-done = bf16[1600,5120]{0,1:T(8,128)(2,1)} async-done(((bf16[1600,320]{0,1:T(8,128)(2,1)}), bf16[1600,5120]{0,1:T(8,128)(2,1)}) %all-gather.5.cloned.1.call-update) | async-done | bytes 16384016 | tf_op jit(solution)/shard_map/all_gather | solution.py:24
  357.5 11.8 %fusion.2 = bf16[1600,320]{0,1:T(8,128)(2,1)} fusion(bf16[1600,5120]{0,1:T(8,128)(2,1)} %all-gather.5.cloned.1.call-done, bf16[1600,320]{0,1:T(8,128)(2,1)} %fusion.3, bf16[1600,320]{0,1:T(8,128)(2,1)} %param.1, bf16[5120,320]{0,1:T(8,128)(2,1)S(1)} %all-reduce.1), kind=kOutput, calls=%fused_computation.3 | convolution fusion | flops 5247488000 | bytes 22732800 | tf_op jit(solution)/shard_map/dot_general | solution.py:23
Async XLA Ops:
  6.5 99.1 %all-gather.3.cloned.1.call-start = ((), (), s32[]{:S(2)}) async-start(), calls=%async_computation | async-start | bytes 18104320 | tf_op jit(solution)/shard_map/all_gather | solution.py:16
  7.3 350.3 %all-gather.5.cloned.1.call-start = ((), (), s32[]{:S(2)}) async-start(), calls=%async_computation.1 | async-start | bytes 18104320 | tf_op jit(solution)/shard_map/all_gather | solution.py:24
Sparse Core Ops, SparseCore 0:
  9.1 96.5 all-gather.2
  266.3 91.1 all-gather.4
where the time goes:
time: 376 us
  waiting for transfers between devices  190 us (51%)
  blocking collectives  138 us (37%)
  matrix products  34.3 us (9%)
  between operations  13.4 us (4%)
    psum x1, blocking collectives, shards(): summed = lax.psum(partial_value, 'fsdp')  138 us
    all_gather x1, waiting for transfers between devices, shards(): gathered = lax.all_gather(iterate, 'tensor', axis=1, tiled=True)  98.3 us
    all_gather x1, waiting for transfers between devices, shards(): lax.all_gather(first_product, 'tensor', axis=1, tiled=True)  91.3 us
    dot_general x1, matrix products, shards(): jnp.dot(lax.all_gather(first_product, 'tensor', axis=1, tiled=True), gram...  11.8 us
    dot_general x1, matrix products, transposed_product(): lax.dot_general(left, right, (((0,), (0,)), ((), ())), preferred_element_...  11.7 us
    dot_general x1, matrix products, shards(): jnp.dot(gathered, gram_panel, preferred_element_type=jnp.float32)  10.8 us
  transfers between devices with their start and end apart: 2, of which 2 were waited for; matrix products, arithmetic and copies ran while one was open for 0% of the time, Pallas kernels for 0%

commit v1 on v0

v1 whole, which is shorter than its diff:
```python
import jax
import jax.numpy as jnp
from jax import lax
from jax.sharding import PartitionSpec as P

ROWS = 12800


def transposed_product(left, right):
    return lax.dot_general(
        left, right, (((0,), (0,)), ((), ())), preferred_element_type=jnp.float32
    )


def shards(iterate):
    gathered = lax.all_gather(iterate, "tensor", axis=1, tiled=True)
    partial = transposed_product(gathered, iterate).astype(jnp.bfloat16)
    block = lax.psum_scatter(partial, "fsdp", scatter_dimension=0, tiled=True)
    columns = lax.all_gather(block, "fsdp", axis=0, tiled=True)
    rows = lax.all_gather(block, "tensor", axis=1, tiled=True)
    square = jnp.dot(rows, columns, preferred_element_type=jnp.float32)
    poly = (2.0315 * square - 4.775 * block.astype(jnp.float32)).astype(jnp.bfloat16)
    panel = lax.all_gather(poly, "fsdp", axis=0, tiled=True)
    product = jnp.dot(gathered, panel, preferred_element_type=jnp.float32)
    factor = 0.2 * ROWS**0.5
    return (factor * (3.4445 * iterate.astype(jnp.float32) + product)).astype(jnp.bfloat16)


def solution(mesh):
    placed = (P("fsdp", "tensor"),)
    return jax.shard_map(
        shards, mesh=mesh, in_specs=placed, out_specs=P("fsdp", "tensor"), check_vma=False
    )
```

time: 376 us -> 404 us (1.074)
  waiting for transfers between devices: 190 us -> 354 us
  blocking collectives: 138 us -> 0 us
  local copies, waits for them, and re-layouts: 0 us -> 5.64 us
    psum x1 -> x0, blocking collectives: 138 us -> none  [shards(): summed = lax.psum(partial_value, 'fsdp')]
    unnamed x2 -> x6, waiting for transfers between devices: 0.73 us -> 84.3 us
    all_gather x1 -> x3, waiting for transfers between devices: 91.3 us -> 172 us  [the longest x1 64.1 us: shards(): panel = lax.all_gather(poly, 'fsdp', axis=0, tiled=True)]
    unnamed x0 -> x4, local copies, waits for them, and re-layouts: none -> 5.64 us
  transfers between devices with their start and end apart: 2 -> 5, of which waited for: 2 -> 5; matrix products, arithmetic and copies ran while one was open for 0% -> 0% of each run, Pallas kernels for 0% -> 0%
where the time goes in v1:
time: 404 us
  waiting for transfers between devices  354 us (88%)
  matrix products  30.7 us (8%)
  between operations  13.2 us (3%)
  local copies, waits for them, and re-layouts  5.64 us (1%)
    all_gather x1, waiting for transfers between devices, shards(): gathered = lax.all_gather(iterate, 'tensor', axis=1, tiled=True)  98.3 us
    unnamed x6, waiting for transfers between devices  84.3 us
    all_gather x1, waiting for transfers between devices, shards(): panel = lax.all_gather(poly, 'fsdp', axis=0, tiled=True)  64.1 us
    all_gather x1, waiting for transfers between devices, shards(): columns = lax.all_gather(block, 'fsdp', axis=0, tiled=True)  63.6 us
    all_gather x1, waiting for transfers between devices, shards(): rows = lax.all_gather(block, 'tensor', axis=1, tiled=True)  44.1 us
    dot_general x1, matrix products, shards(): product = jnp.dot(gathered, panel, preferred_element_type=jnp.float32)  13.5 us
    dot_general x1, matrix products, transposed_product(): lax.dot_general(left, right, (((0,), (0,)), ((), ())), preferred_element_...  9.99 us
  transfers between devices with their start and end apart: 5, of which 5 were waited for; matrix products, arithmetic and copies ran while one was open for 0% of the time, Pallas kernels for 0%

profile of v1, /device:TPU:1, one launch (start us, length us, event | category | flops | bytes accessed | tf_op | source)
XLA Modules:
  0.0 404.1 jit_solution(5562512746322161327)
XLA Ops:
  6.5 0.0 all-gather.5.cloned.1.call-start
  6.5 0.7 all-gather.5.cloned.1.call-update
  7.3 0.0 reduce-scatter.4.cloned.1.call-start
  7.3 98.3 %all-gather.5.cloned.1.call-done = bf16[1600,5120]{0,1:T(8,128)(2,1)} async-done(((bf16[1600,320]{0,1:T(8,128)(2,1)}), bf16[1600,5120]{0,1:T(8,128)(2,1)}) %all-gather.5.cloned.1.call-update) | async-done | bytes 16384016 | tf_op jit(solution)/shard_map/all_gather | solution.py:16
  105.6 10.0 %convolution_convert_fusion = bf16[5120,320]{0,1:T(8,128)(2,1)S(1)} fusion(bf16[1600,5120]{0,1:T(8,128)(2,1)} %all-gather.5.cloned.1.call-done, bf16[1600,320]{0,1:T(8,128)(2,1)} %param.1), kind=kOutput, calls=%fused_computation | convolution fusion | flops 5244518400 | bytes 20684800 | tf_op jit(solution)/shard_map/dot_general | solution.py:10
  115.6 3.7 copy.2
  119.3 0.0 reduce-scatter.4.cloned.1.call-update
  119.3 0.0 all-gather.9.cloned.1.call-start
  119.4 83.1 %reduce-scatter.4.cloned.1.call-done = bf16[640,320]{1,0:T(8,128)(2,1)} async-done(((bf16[5120,320]{1,0:T(8,128)(2,1)}), bf16[640,320]{1,0:T(8,128)(2,1)}) %reduce-scatter.4.cloned.1.call-update) | async-done | bytes 409616
  202.4 2.0 copy.3
  204.4 0.0 all-gather.9.cloned.1.call-update
  204.4 0.0 all-gather.7.cloned.1.call-start
  204.5 0.5 all-gather.7.cloned.1.call-update
  205.0 0.0 copy-start
  205.0 0.0 all-gather.11.cloned.1.call-start
  205.1 63.6 %all-gather.9.cloned.1.call-done = bf16[5120,320]{0,1:T(8,128)(2,1)} async-done(((bf16[640,320]{0,1:T(8,128)(2,1)}), bf16[5120,320]{0,1:T(8,128)(2,1)}) %all-gather.9.cloned.1.call-update) | async-done | bytes 3276816 | tf_op jit(solution)/shard_map/all_gather | solution.py:19
  268.7 44.1 %all-gather.7.cloned.1.call-done = bf16[640,5120]{0,1:T(8,128)(2,1)} async-done(((bf16[640,320]{0,1:T(8,128)(2,1)}), bf16[640,5120]{0,1:T(8,128)(2,1)}) %all-gather.7.cloned.1.call-update) | async-done | bytes 6553616 | tf_op jit(solution)/shard_map/all_gather | solution.py:20
  312.7 7.3 %fusion.4 = bf16[640,320]{0,1:T(8,128)(2,1)} fusion(bf16[5120,320]{0,1:T(8,128)(2,1)} %all-gather.9.cloned.1.call-done, bf16[640,5120]{0,1:T(8,128)(2,1)} %all-gather.7.cloned.1.call-done, bf16[640,320]{0,1:T(8,128)(2,1)} %copy.3), kind=kOutput, calls=%fused_computation.7 | convolution fusion | flops 2098176000 | bytes 10649600 | tf_op jit(solution)/shard_map/dot_general | solution.py:21
  320.0 0.0 all-gather.11.cloned.1.call-update
  320.0 64.1 %all-gather.11.cloned.1.call-done = bf16[5120,320]{0,1:T(8,128)(2,1)} async-done(((bf16[640,320]{0,1:T(8,128)(2,1)}), bf16[5120,320]{0,1:T(8,128)(2,1)}) %all-gather.11.cloned.1.call-update) | async-done | bytes 3276816 | tf_op jit(solution)/shard_map/all_gather | solution.py:23
  384.1 0.0 copy-done
  384.1 13.5 %fusion.2 = bf16[1600,320]{0,1:T(8,128)(2,1)} fusion(bf16[5120,320]{0,1:T(8,128)(2,1)} %all-gather.11.cloned.1.call-done, bf16[1600,5120]{0,1:T(8,128)(2,1)} %all-gather.5.cloned.1.call-done, bf16[1600,320]{0,1:T(8,128)(2,1)S(1)} %copy-done), kind=kOutput, calls=%fused_computation.4 | convolution fusion | flops 5245440000 | bytes 21708800 | tf_op jit(solution)/shard_map/dot_general | solution.py:24
Async XLA Ops:
  6.5 99.1 %all-gather.5.cloned.1.call-start = ((), (), s32[]{:S(2)}) async-start(), calls=%async_computation.1 | async-start | bytes 18104320 | tf_op jit(solution)/shard_map/all_gather | solution.py:16
  7.3 195.2 %reduce-scatter.4.cloned.1.call-start = ((), (), s32[]{:S(2)}) async-start(), calls=%async_computation.5 | async-start | bytes 4423680
  119.3 149.3 %all-gather.9.cloned.1.call-start = ((), (), s32[]{:S(2)}) async-start(), calls=%async_computation.3 | async-start | bytes 3686400 | tf_op jit(solution)/shard_map/all_gather | solution.py:19
  204.4 108.3 %all-gather.7.cloned.1.call-start = ((), (), s32[]{:S(2)}) async-start(), calls=%async_computation.2 | async-start | bytes 6963200 | tf_op jit(solution)/shard_map/all_gather | solution.py:20
  205.0 179.1 %copy-start = (bf16[1600,320]{0,1:T(8,128)(2,1)S(1)}, bf16[1600,320]{0,1:T(8,128)(2,1)}, u32[]{:S(2)}) copy-start(bf16[1600,320]{0,1:T(8,128)(2,1)} %param.1) | copy-start | bytes 3072004
  205.0 179.1 %all-gather.11.cloned.1.call-start = ((), (), s32[]{:S(2)}) async-start(), calls=%async_computation.4 | async-start | bytes 3686400 | tf_op jit(solution)/shard_map/all_gather | solution.py:23
Sparse Core Ops, SparseCore 0:
  9.1 96.5 all-gather.4
  119.4 82.9 reduce-scatter.3
  205.0 63.5 all-gather.8
  270.3 42.3 all-gather.6
  320.1 63.9 all-gather.10

commit v2 on v1

v2 whole, which is shorter than its diff:
```python
import functools

import jax
import jax.numpy as jnp
from jax import lax
from jax.experimental import pallas as pl
from jax.experimental.pallas import tpu as pltpu
from jax.sharding import PartitionSpec as P

MESH = pl.DeviceIdType.MESH
BF16, F32 = jnp.bfloat16, jnp.float32
ROWS = 12800
FACTOR = 0.2 * ROWS**0.5
A, B, C = 3.4445, -4.775, 2.0315


class Where:
    def __init__(self):
        f, t = lax.axis_index("fsdp"), lax.axis_index("tensor")
        self.zh, self.x = f // 4, f % 4
        self.y, self.zl, self.c = t // 4, (t // 2) % 2, t % 2

    def device(self, dx=0, dzh=0, dy=0, dzl=0, dc=0):
        x, y = (self.x + dx) % 4, (self.y + dy) % 4
        zh, zl, c = (self.zh + dzh) % 2, (self.zl + dzl) % 2, (self.c + dc) % 2
        return (zh * 4 + x, y * 4 + zl * 2 + c)

    def tslot(self, d, dz):
        return (self.y + d) % 4 * 2 + (self.zl + dz) % 2

    def fslot(self, d, dz):
        return (self.x + d) % 4 * 2 + (self.zh + dz) % 2


class Gather:
    def __init__(self, view, slot, device, send, recv, twice):
        self.view, self.slot, self.device, self.send, self.recv = view, slot, device, send, recv
        ring_p, ring_m, pair = (1, 0), (-1, 0), (0, 1)
        if twice:
            self.plan = {
                "ap": ((0, 0), ring_p, None), "am": ((0, 0), ring_m, None), "az": ((0, 0), pair, None),
                "bm": ((1, 0), ring_m, None), "bz": ((1, 0), pair, None), "bp": ((0, 1), ring_p, None),
                "cp": ((-1, 1), ring_p, 0), "cm": ((1, 1), ring_m, 1),
            }
            self.after = {"am": ("bm", "bz"), "az": ("bp",), "bp": ("cp",), "bz": ("cm",)}
            self.order = [("az",), ("am",), ("ap",), ("bp",), ("bz",), ("bm",), ("cp", "cm")]
        else:
            self.plan = {
                "ap": ((0, 0), ring_p, None), "am": ((0, 0), ring_m, None), "az": ((0, 0), pair, None),
                "bp": ((0, 1), ring_p, None), "bm": ((0, 1), ring_m, None),
                "cp": ((-1, 0), ring_p, 0), "cm": ((1, 0), ring_m, 1),
                "dp": ((-1, 1), ring_p, 0), "dm": ((1, 1), ring_m, 1),
            }
            self.after = {"az": ("bp", "bm"), "ap": ("cp",), "am": ("cm",), "bp": ("dp",), "bm": ("dm",)}
            self.order = [("az",), ("ap",), ("am",), ("bp",), ("bm",), ("cp", "cm"), ("dp", "dm")]
        self.names = list(self.plan)

    def copy(self, name, receiving):
        (d, dz), (step, flip), half = self.plan[name]
        if receiving:
            d, dz = d - step, (dz + flip) % 2
        i = self.names.index(name)
        ref = self.view(self.slot(d, dz), half)
        return pltpu.make_async_remote_copy(
            src_ref=ref, dst_ref=ref, send_sem=self.send.at[i], recv_sem=self.recv.at[i],
            device_id=self.device(step, flip), device_id_type=MESH,
        )

    def start(self, name):
        self.copy(name, False).start()

    def begin(self):
        for name in ("az", "am", "ap"):
            self.start(name)

    def take(self, names):
        for name in names:
            self.copy(name, True).wait_recv()
            for nxt in self.after.get(name, ()):
                self.start(nxt)
        (d, dz), (step, flip), _ = self.plan[names[0]]
        return d - step, (dz + flip) % 2

    def end(self):
        for name in self.names:
            self.copy(name, False).wait_send()


def kernel(
    x_ref, o_ref, xin, xb, gp, crecv, own, rsst, rsrecv, rzst, rzrecv, ga, gc, pc, acc, uo, urecv,
    ts, tr, gs, gr, hs, hr, ps, pr, xs, xr, cs, cr, rss, rsr, zs, zr, shs, shr, pss, psr, us, ur,
):
    w = Where()
    c = w.c
    rows, width = x_ref.shape
    half, full = rows // 2, 2 * width
    mate = w.device(dc=1)

    peers = [dict(dc=1), dict(dy=1), dict(dy=-1), dict(dzl=1), dict(dx=1), dict(dx=-1), dict(dx=2), dict(dzh=1)]
    barrier = pltpu.get_barrier_semaphore()
    for peer in peers:
        pl.semaphore_signal(barrier, inc=1, device_id=w.device(**peer), device_id_type=MESH)
    pl.semaphore_wait(barrier, len(peers))

    def remote(src, dst, send, recv, device):
        return pltpu.make_async_remote_copy(
            src_ref=src, dst_ref=dst, send_sem=send, recv_sem=recv, device_id=device, device_id_type=MESH
        )

    swap = remote(x_ref.at[pl.ds((1 - c) * half, half), :], xin, xs, xr, mate)
    swap.start()
    mine = w.tslot(0, 0)
    swap.wait_recv()
    step_rows = half // 5

    def join(i, _):
        at = pl.ds(i * step_rows, step_rows)
        kept, got = x_ref[pl.ds(c * half + i * step_rows, step_rows), :], xin[at, :]
        first = c == 0
        xb[mine, at, :] = jnp.concatenate([jnp.where(first, kept, got), jnp.where(first, got, kept)], axis=1)
        return 0

    lax.fori_loop(0, 5, join, 0)

    def tdevice(step, flip):
        return w.device(dy=step, dzl=flip)

    def fdevice(step, flip):
        return w.device(dx=step, dzh=flip)

    def xview(slot, part):
        if part is None:
            return xb.at[slot]
        return xb.at[slot, pl.ds(part * (half // 2), half // 2), :]

    gx = Gather(xview, w.tslot, tdevice, ts, tr, True)
    gx.begin()
    kept_rows = pl.ds(c * width, width)
    other_rows = pl.ds((1 - c) * width, width)

    def gram(step, rel):
        slot = w.tslot(*rel)
        buf = step % 2

        def tile(i, _):
            at = pl.ds(pl.multiple_of(i * 128, 128), 128)
            gp[buf, at, :] = lax.dot_general(
                xb[slot, :, at], xb[mine], (((0,), (0,)), ((), ())), preferred_element_type=F32
            )
            return 0

        lax.fori_loop(0, full // 128, tile, 0)
        remote(gp.at[buf, other_rows, :], crecv.at[step], cs.at[step], cr.at[step], mate).start()

    def scatter(step, rel):
        buf = step % 2
        cp = remote(gp.at[buf, other_rows, :], crecv.at[step], cs.at[step], cr.at[step], mate)
        cp.wait_recv()
        total = gp[buf, kept_rows, :] + crecv[step]
        cp.wait_send()
        to_x, to_zh = (w.y + rel[0]) % 4, (w.zl + rel[1]) % 2
        away = (to_x - w.x + 4) % 4

        @pl.when(away == 0)
        def _():
            own[to_zh] = total

        @pl.when(away != 0)
        def _():
            rsst[step] = total.astype(BF16)
            remote(
                rsst.at[step], rsrecv.at[to_zh, away - 1], rss.at[step], rsr.at[to_zh, away - 1],
                w.device(dx=away),
            ).start()

    steps = [(0, 0)]
    gram(0, (0, 0))
    for names in gx.order:
        rel = gx.take(names)
        gram(len(steps), rel)
        scatter(len(steps) - 1, steps[-1])
        steps.append(rel)
    scatter(7, steps[-1])

    def received(zh):
        for i in range(3):
            remote(rsst.at[0], rsrecv.at[zh, i], rss.at[0], rsr.at[zh, i], mate).wait_recv()
        return own[zh] + rsrecv[zh, 0].astype(F32) + rsrecv[zh, 1].astype(F32) + rsrecv[zh, 2].astype(F32)

    across = remote(rzst, rzrecv, zs, zr, w.device(dzh=1))
    rzst[...] = received(1 - w.zh).astype(BF16)
    across.start()
    own[w.zh] = received(w.zh)
    across.wait_recv()
    block = (own[w.zh] + rzrecv[...].astype(F32)).astype(BF16)

    fmine = w.fslot(0, 0)
    ga[mine] = block
    gc[fmine, kept_rows, :] = block

    def rows_of(buf):
        def view(slot, part):
            if part is None:
                return buf.at[slot, kept_rows, :]
            return buf.at[slot, pl.ds(c * width + part * (width // 2), width // 2), :]

        return view

    def aview(slot, part):
        if part is None:
            return ga.at[slot]
        return ga.at[slot, pl.ds(part * (width // 2), width // 2), :]

    def share(buf, slot, send, recv):
        ref = buf.at[slot, kept_rows, :]
        return remote(ref, ref, send.at[slot], recv.at[slot], mate)

    def shared(buf, slot, send, recv):
        ref = buf.at[slot, other_rows, :]
        return remote(ref, ref, send.at[slot], recv.at[slot], mate)

    ggc = Gather(rows_of(gc), w.fslot, fdevice, gs, gr, False)
    gga = Gather(aview, w.tslot, tdevice, hs, hr, True)
    ggc.begin()
    gga.begin()
    share(gc, fmine, shs, shr).start()
    for na, nc in zip(gga.order, ggc.order):
        gga.take(na)
        rel = ggc.take(nc)
        share(gc, w.fslot(*rel), shs, shr).start()
    for j in range(8):
        shared(gc, j, shs, shr).wait_recv()

    def square(j, total):
        return total + jnp.dot(ga[j], gc[j], preferred_element_type=F32)

    total = lax.fori_loop(0, 8, square, jnp.zeros((width, full), F32))
    pc[fmine, kept_rows, :] = (C * total + B * ga[mine].astype(F32)).astype(BF16)

    gpc = Gather(rows_of(pc), w.fslot, fdevice, ps, pr, True)
    gpc.begin()
    share(pc, fmine, pss, psr).start()
    tile_rows = half // 5

    def product(slot, first):
        shared(pc, slot, pss, psr).wait_recv()

        def tile(i, _):
            at = pl.ds(pl.multiple_of(i * tile_rows, tile_rows), tile_rows)
            term = jnp.dot(xb[slot, at, :], pc[slot], preferred_element_type=F32)
            if first:
                acc[at, :] = A * xb[mine, at, :].astype(F32) + term
            else:
                acc[at, :] += term
            return 0

        lax.fori_loop(0, 5, tile, 0)

    waiting = fmine
    for i, names in enumerate(gpc.order):
        rel = gpc.take(names)
        slot = w.fslot(*rel)
        share(pc, slot, pss, psr).start()
        product(waiting, i == 0)
        waiting = slot
    product(waiting, False)

    back = remote(uo, urecv, us, ur, mate)

    def split(i, _):
        at = pl.ds(pl.multiple_of(i * tile_rows, tile_rows), tile_rows)
        value = (FACTOR * acc[at, :]).astype(BF16)
        left, right = value[:, :width], value[:, width:]
        first = c == 0
        o_ref[pl.ds(pl.multiple_of(c * half + i * tile_rows, 16), tile_rows), :] = jnp.where(first, left, right)
        uo[at, :] = jnp.where(first, right, left)
        return 0

    lax.fori_loop(0, 5, split, 0)
    back.start()

    swap.wait_send()
    for g in (gx, ggc, gga, gpc):
        g.end()
    for i, rel in enumerate(steps):
        away = ((w.y + rel[0]) % 4 - w.x + 4) % 4

        @pl.when(away != 0)
        def _():
            remote(rsst.at[i], rsrecv.at[0, 0], rss.at[i], rsr.at[0, 0], mate).wait_send()

    across.wait_send()
    for j in range(8):
        share(gc, j, shs, shr).wait_send()
        share(pc, j, pss, psr).wait_send()
    back.wait()
    o_ref[pl.ds((1 - c) * half, half), :] = urecv[...]


def shards(iterate):
    rows, width = iterate.shape
    half, full = rows // 2, 2 * width
    dma = pltpu.SemaphoreType.DMA
    vmem = pltpu.VMEM
    return pl.pallas_call(
        kernel,
        out_shape=jax.ShapeDtypeStruct((rows, width), BF16),
        in_specs=[pl.BlockSpec(memory_space=pltpu.VMEM)],
        out_specs=pl.BlockSpec(memory_space=pltpu.VMEM),
        scratch_shapes=[
            vmem((half, width), BF16),
            vmem((8, half, full), BF16),
            vmem((2, full, full), F32),
            vmem((8, width, full), F32),
            vmem((2, width, full), F32),
            vmem((8, width, full), BF16),
            vmem((2, 3, width, full), BF16),
            vmem((width, full), BF16),
            vmem((width, full), BF16),
            vmem((8, width, full), BF16),
            vmem((8, full, full), BF16),
            vmem((8, full, full), BF16),
            vmem((half, full), F32),
            vmem((half, width), BF16),
            vmem((half, width), BF16),
            dma((8,)), dma((8,)), dma((9,)), dma((9,)), dma((8,)), dma((8,)), dma((8,)), dma((8,)),
            dma, dma, dma((8,)), dma((8,)), dma((8,)), dma((2, 3)), dma, dma,
            dma((8,)), dma((8,)), dma((8,)), dma((8,)), dma, dma,
        ],
        compiler_params=pltpu.CompilerParams(
            collective_id=0, has_side_effects=True, vmem_limit_bytes=60 * 2**20
        ),
        cost_estimate=pl.CostEstimate(flops=6 * rows * width * 16 * width, bytes_accessed=4 * rows * width, transcendentals=0),
        name="newton_schulz",
    )(iterate)


def solution(mesh):
    return jax.shard_map(
        shards, mesh=mesh, in_specs=(P("fsdp", "tensor"),), out_specs=P("fsdp", "tensor"), check_vma=False
    )
```

time: 404 us -> 209 us (0.52)
  waiting for transfers between devices: 354 us -> 0 us
  Pallas kernels: 0 us -> 204 us
  matrix products: 30.7 us -> 0 us
  between operations: 13.2 us -> 0.01 us
    all_gather x4 -> x0, waiting for transfers between devices: 270 us -> none  [the longest x1 98.3 us: shards(): gathered = lax.all_gather(iterate, 'tensor', axis=1, tiled=True)]
    pallas_call x0 -> x1, Pallas kernels: none -> 204 us  [shards(): pl.pallas_call(kernel, out_shape=jax.ShapeDtypeStruct((rows, width), BF16...]
    unnamed x6 -> x0, waiting for transfers between devices: 84.3 us -> none
    dot_general x3 -> x0, matrix products: 30.7 us -> none  [the longest x1 13.5 us: shards(): product = jnp.dot(gathered, panel, preferred_element_type=jnp.float32)]
  transfers between devices with their start and end apart: 5 -> 0, of which waited for: 5 -> 0; matrix products, arithmetic and copies ran while one was open for 0% -> 0% of each run, Pallas kernels for 0% -> 0%
where the time goes in v2:
time: 209 us; the launch traced here: 208 us
  Pallas kernels  204 us (98%)
  local copies, waits for them, and re-layouts  4.82 us (2%)
    pallas_call x1, Pallas kernels, shards(): pl.pallas_call(kernel, out_shape=jax.ShapeDtypeStruct((rows, width), BF16...  204 us

profile of v2, /device:TPU:1, one launch (start us, length us, event | category | flops | bytes accessed | tf_op | source)
XLA Modules:
  0.0 208.4 jit_solution(3327589050637379032)
XLA Ops:
  0.0 2.4 %copy.2.x_ref = bf16[1600,320]{1,0:T(8,128)(2,1)} copy(bf16[1600,320]{0,1:T(8,128)(2,1)} %param.1) | data formatting | bytes 2048000 | tf_op args[0]
  2.4 203.6 %newton_schulz.1 = bf16[1600,320]{1,0:T(8,128)(2,1)} custom-call(bf16[1600,320]{1,0:T(8,128)(2,1)} %copy.2.x_ref), custom_call_target="tpu_custom_call" | custom-call | flops 15728640000 | bytes 2048000 | tf_op jit(solution)/shard_map/newton_schulz/pallas_call | solution.py:305
  206.0 2.4 %copy.3 = bf16[1600,320]{0,1:T(8,128)(2,1)} copy(bf16[1600,320]{1,0:T(8,128)(2,1)} %newton_schulz.1) | data formatting | bytes 2048000 | tf_op jit(solution)/shard_map/newton_schulz/pallas_call | solution.py:305

commit v3 on v2

v3 whole, which is shorter than its diff:
```python
import functools

import jax
import jax.numpy as jnp
from jax import lax
from jax.experimental import pallas as pl
from jax.experimental.pallas import tpu as pltpu
from jax.sharding import PartitionSpec as P

MESH = pl.DeviceIdType.MESH
BF16, F32 = jnp.bfloat16, jnp.float32
ROWS = 12800
FACTOR = 0.2 * ROWS**0.5
A, B, C = 3.4445, -4.775, 2.0315
X_CHUNKS, G_CHUNKS = 1, 1


class Where:
    def __init__(self):
        f, t = lax.axis_index("fsdp"), lax.axis_index("tensor")
        self.zh, self.x = f // 4, f % 4
        self.y, self.zl, self.c = t // 4, (t // 2) % 2, t % 2

    def device(self, dx=0, dzh=0, dy=0, dzl=0, dc=0):
        x, y = (self.x + dx) % 4, (self.y + dy) % 4
        zh, zl, c = (self.zh + dzh) % 2, (self.zl + dzl) % 2, (self.c + dc) % 2
        return (zh * 4 + x, y * 4 + zl * 2 + c)

    def tslot(self, d, dz):
        return (self.y + d) % 4 * 2 + (self.zl + dz) % 2

    def fplace(self, d, dz):
        return (self.x + d) % 4, (self.zh + dz) % 2


class Gather:
    def __init__(self, chunks, view, slot, device, send, recv, twice):
        self.chunks, self.view, self.slot, self.device, self.send, self.recv = chunks, view, slot, device, send, recv
        ring_p, ring_m, pair = (1, 0), (-1, 0), (0, 1)
        if twice:
            self.plan = {
                "ap": ((0, 0), ring_p, None), "am": ((0, 0), ring_m, None), "az": ((0, 0), pair, None),
                "bm": ((1, 0), ring_m, None), "bz": ((1, 0), pair, None), "bp": ((0, 1), ring_p, None),
                "cp": ((-1, 1), ring_p, 0), "cm": ((1, 1), ring_m, 1),
            }
            self.after = {"am": ("bm", "bz"), "az": ("bp",), "bp": ("cp",), "bz": ("cm",)}
            self.order = [("az",), ("am",), ("ap",), ("bp",), ("bz",), ("bm",), ("cp", "cm")]
        else:
            self.plan = {
                "ap": ((0, 0), ring_p, None), "am": ((0, 0), ring_m, None), "az": ((0, 0), pair, None),
                "bp": ((0, 1), ring_p, None), "bm": ((0, 1), ring_m, None),
                "cp": ((-1, 0), ring_p, 0), "cm": ((1, 0), ring_m, 1),
                "dp": ((-1, 1), ring_p, 0), "dm": ((1, 1), ring_m, 1),
            }
            self.after = {"az": ("bp", "bm"), "ap": ("cp",), "am": ("cm",), "bp": ("dp",), "bm": ("dm",)}
            self.order = [("az",), ("ap",), ("am",), ("bp",), ("bm",), ("cp", "cm"), ("dp", "dm")]
        self.names = list(self.plan)

    def copy(self, name, chunk, receiving):
        (d, dz), (step, flip), part = self.plan[name]
        if receiving:
            d, dz = d - step, (dz + flip) % 2
        i = self.names.index(name)
        ref = self.view(self.slot(d, dz), chunk, part)
        return pltpu.make_async_remote_copy(
            src_ref=ref, dst_ref=ref, send_sem=self.send.at[chunk, i], recv_sem=self.recv.at[chunk, i],
            device_id=self.device(step, flip), device_id_type=MESH,
        )

    def begin(self):
        for chunk in range(self.chunks):
            for name in ("az", "am", "ap"):
                self.copy(name, chunk, False).start()

    def take(self, names):
        for chunk in range(self.chunks):
            for name in names:
                self.copy(name, chunk, True).wait_recv()
                for nxt in self.after.get(name, ()):
                    self.copy(nxt, chunk, False).start()
        (d, dz), (step, flip), _ = self.plan[names[0]]
        return d - step, (dz + flip) % 2

    def end(self):
        for chunk in range(self.chunks):
            for name in self.names:
                self.copy(name, chunk, False).wait_send()


def kernel(
    x_ref, o_ref, xin, xb, gp, crecv, own, rsst, rsrecv, rzst, rzrecv, ga, gc, pc, acc, uo, urecv,
    ts, tr, gs, gr, hs, hr, ps, pr, xs, xr, cs, cr, rss, rsr, zs, zr, shs, shr, pss, psr, us, ur,
):
    w = Where()
    c = w.c
    rows, width = x_ref.shape
    half, full, quarter = rows // 2, 2 * width, width // 4
    mate = w.device(dc=1)

    peers = [dict(dc=1), dict(dy=1), dict(dy=-1), dict(dzl=1), dict(dx=1), dict(dx=-1), dict(dx=2), dict(dzh=1)]
    barrier = pltpu.get_barrier_semaphore()
    for peer in peers:
        pl.semaphore_signal(barrier, inc=1, device_id=w.device(**peer), device_id_type=MESH)
    pl.semaphore_wait(barrier, len(peers))

    def remote(src, dst, send, recv, device):
        return pltpu.make_async_remote_copy(
            src_ref=src, dst_ref=dst, send_sem=send, recv_sem=recv, device_id=device, device_id_type=MESH
        )

    swap = remote(x_ref.at[pl.ds((1 - c) * half, half), :], xin, xs, xr, mate)
    swap.start()
    mine = w.tslot(0, 0)
    swap.wait_recv()
    step_rows = half // 5

    def join(i, _):
        at = pl.ds(i * step_rows, step_rows)
        kept, got = x_ref[pl.ds(c * half + i * step_rows, step_rows), :], xin[at, :]
        first = c == 0
        xb[mine, at, :] = jnp.concatenate([jnp.where(first, kept, got), jnp.where(first, got, kept)], axis=1)
        return 0

    lax.fori_loop(0, 5, join, 0)

    def tdevice(step, flip):
        return w.device(dy=step, dzl=flip)

    def fdevice(step, flip):
        return w.device(dx=step, dzh=flip)

    chunk_rows = half // X_CHUNKS
    part_rows = (chunk_rows // 32 + 1) * 16

    def xview(slot, chunk, part):
        at, size = ((0, chunk_rows), (0, part_rows), (part_rows, chunk_rows - part_rows))[0 if part is None else part + 1]
        return xb.at[slot, pl.ds(chunk * chunk_rows + at, size), :]

    gx = Gather(X_CHUNKS, xview, w.tslot, tdevice, ts, tr, True)
    gx.begin()
    kept_rows = pl.ds(c * width, width)
    other_rows = pl.ds((1 - c) * width, width)

    def gram(step, rel):
        slot = w.tslot(*rel)
        buf = step % 2

        gp[buf] = lax.dot_general(xb[slot], xb[mine], (((0,), (0,)), ((), ())), preferred_element_type=F32)
        remote(gp.at[buf, other_rows, :], crecv.at[step], cs.at[step], cr.at[step], mate).start()

    def scatter(step, rel):
        buf = step % 2
        cp = remote(gp.at[buf, other_rows, :], crecv.at[step], cs.at[step], cr.at[step], mate)
        cp.wait_recv()
        total = gp[buf, kept_rows, :] + crecv[step]
        cp.wait_send()
        own[w.tslot(*rel)] = gp_quarter(buf, step)
        rsst[step] = total.astype(BF16)
        for d in (1, 2, 3):
            x_copy(step, rel, d).start()

    def gp_quarter(buf, step):
        return gp[buf, pl.ds(c * width + w.x * quarter, quarter), :] + crecv[step, pl.ds(w.x * quarter, quarter), :]

    def x_copy(step, rel, d):
        to = (w.x + d) % 4
        slot = w.tslot(*rel)
        return remote(
            rsst.at[step, pl.ds(to * quarter, quarter), :], rsrecv.at[d - 1, slot],
            rss.at[step, d - 1], rsr.at[d - 1, slot], w.device(dx=d),
        )

    def z_copy(rel):
        at = (w.y + rel[0]) % 4
        return remote(rzst.at[at], rzrecv.at[at], zs.at[at], zr.at[at], w.device(dzh=1))

    def summed(step, rel):
        slot = w.tslot(*rel)
        for d in (1, 2, 3):
            x_copy(step, rel, d).wait_recv()
        total = own[slot] + sum(rsrecv[d, slot].astype(F32) for d in range(3))
        there = (w.zl + rel[1]) % 2 != w.zh

        @pl.when(there)
        def _():
            rzst[(w.y + rel[0]) % 4] = total.astype(BF16)
            z_copy(rel).start()

        @pl.when(jnp.logical_not(there))
        def _():
            own[slot] = total

    steps = [(0, 0)]
    gram(0, (0, 0))
    for names in gx.order:
        rel = gx.take(names)
        gram(len(steps), rel)
        scatter(len(steps) - 1, steps[-1])
        if len(steps) > 2:
            summed(len(steps) - 3, steps[-3])
        steps.append(rel)
    scatter(7, steps[-1])
    for i in (5, 6, 7):
        summed(i, steps[i])

    kept_quarter = pl.ds(c * width + w.x * quarter, quarter)
    for i in range(4):
        z_copy((i, w.zh - w.zl + 2)).wait_recv()
        at = (w.y + i) % 4
        block = (own[at * 2 + w.zh] + rzrecv[at].astype(F32)).astype(BF16)
        ga[mine, at] = block
        gc[at, w.zh, kept_quarter, :] = block

    def which_of(chunk, part):
        size = 4 // G_CHUNKS
        return (chunk * size, size) if part is None else (chunk * size + part * (size // 2), size // 2)

    def rows_of(buf):
        def view(place, chunk, part):
            x, zh = place
            which = pl.ds(*which_of(chunk, part))
            return buf.at[which, zh, pl.ds(c * width + x * quarter, quarter), :]

        return view

    def aview(slot, chunk, part):
        return ga.at[slot, pl.ds(*which_of(chunk, part))]

    def share(buf, place, send, recv):
        x, zh = place
        ref = buf.at[:, zh, pl.ds(c * width + x * quarter, quarter), :]
        return remote(ref, ref, send.at[x * 2 + zh], recv.at[x * 2 + zh], mate)

    def shared(buf, place, send, recv):
        x, zh = place
        ref = buf.at[:, zh, pl.ds((1 - c) * width + x * quarter, quarter), :]
        return remote(ref, ref, send.at[x * 2 + zh], recv.at[x * 2 + zh], mate)

    fmine = w.fplace(0, 0)
    ggc = Gather(G_CHUNKS, rows_of(gc), w.fplace, fdevice, gs, gr, False)
    gga = Gather(G_CHUNKS, aview, w.tslot, tdevice, hs, hr, True)
    ggc.begin()
    gga.begin()
    share(gc, fmine, shs, shr).start()
    for na, nc in zip(gga.order, ggc.order):
        gga.take(na)
        rel = ggc.take(nc)
        share(gc, w.fplace(*rel), shs, shr).start()
    for j in range(8):
        shared(gc, (j // 2, j % 2), shs, shr).wait_recv()

    total = jnp.dot(
        jnp.concatenate([ga[j].reshape(width, full) for j in range(8)], axis=1),
        gc[...].reshape(8 * full, full), preferred_element_type=F32,
    )
    value = (C * total + B * ga[mine].reshape(width, full).astype(F32)).astype(BF16)
    for i in range(4):
        pc[i, w.zh, kept_quarter, :] = value[i * quarter:(i + 1) * quarter]

    gpc = Gather(G_CHUNKS, rows_of(pc), w.fplace, fdevice, ps, pr, True)
    gpc.begin()
    share(pc, fmine, pss, psr).start()
    tile_rows = half // 5

    def product(zh, first):
        for x in range(4):
            shared(pc, (x, zh), pss, psr).wait_recv()

        left = jnp.concatenate([xb[j * 2 + zh] for j in range(4)], axis=1)
        for at in range(0, full, 256):
            cols = pl.ds(at, min(256, full - at))
            right = jnp.concatenate([pc[j, zh, :, cols] for j in range(4)], axis=0)
            start = A * xb[mine, :, cols].astype(F32) if first else acc[:, cols]
            acc[:, cols] = start + jnp.dot(left, right, preferred_element_type=F32)

    for names in gpc.order:
        if names == ("cp", "cm"):
            product(w.zh, True)
        share(pc, w.fplace(*gpc.take(names)), pss, psr).start()
    product(1 - w.zh, False)

    back = remote(uo, urecv, us, ur, mate)

    def split(i, _):
        at = pl.ds(pl.multiple_of(i * tile_rows, tile_rows), tile_rows)
        value = (FACTOR * acc[at, :]).astype(BF16)
        left, right = value[:, :width], value[:, width:]
        first = c == 0
        o_ref[pl.ds(pl.multiple_of(c * half + i * tile_rows, 16), tile_rows), :] = jnp.where(first, left, right)
        uo[at, :] = jnp.where(first, right, left)
        return 0

    lax.fori_loop(0, 5, split, 0)
    back.start()

    swap.wait_send()
    for g in (gx, ggc, gga, gpc):
        g.end()
    for i, rel in enumerate(steps):
        for d in (1, 2, 3):
            x_copy(i, rel, d).wait_send()
    for i in range(4):
        z_copy((i, 0)).wait_send()
    for j in range(8):
        share(gc, (j // 2, j % 2), shs, shr).wait_send()
        share(pc, (j // 2, j % 2), pss, psr).wait_send()
    back.wait()
    o_ref[pl.ds((1 - c) * half, half), :] = urecv[...]


def shards(iterate):
    rows, width = iterate.shape
    half, full, quarter = rows // 2, 2 * width, width // 4
    dma = pltpu.SemaphoreType.DMA
    vmem = pltpu.VMEM
    return pl.pallas_call(
        kernel,
        out_shape=jax.ShapeDtypeStruct((rows, width), BF16),
        in_specs=[pl.BlockSpec(memory_space=pltpu.VMEM)],
        out_specs=pl.BlockSpec(memory_space=pltpu.VMEM),
        scratch_shapes=[
            vmem((half, width), BF16),
            vmem((8, half, full), BF16),
            vmem((2, full, full), F32),
            vmem((8, width, full), F32),
            vmem((8, quarter, full), F32),
            vmem((8, width, full), BF16),
            vmem((3, 8, quarter, full), BF16),
            vmem((4, quarter, full), BF16),
            vmem((4, quarter, full), BF16),
            vmem((8, 4, quarter, full), BF16),
            vmem((4, 2, full, full), BF16),
            vmem((4, 2, full, full), BF16),
            vmem((half, full), F32),
            vmem((half, width), BF16),
            vmem((half, width), BF16),
            dma((X_CHUNKS, 8)), dma((X_CHUNKS, 8)), dma((G_CHUNKS, 9)), dma((G_CHUNKS, 9)),
            dma((G_CHUNKS, 8)), dma((G_CHUNKS, 8)), dma((G_CHUNKS, 8)), dma((G_CHUNKS, 8)),
            dma, dma, dma((8,)), dma((8,)), dma((8, 3)), dma((3, 8)), dma((4,)), dma((4,)),
            dma((8,)), dma((8,)), dma((8,)), dma((8,)), dma, dma,
        ],
        compiler_params=pltpu.CompilerParams(
            collective_id=0, has_side_effects=True, vmem_limit_bytes=60 * 2**20
        ),
        cost_estimate=pl.CostEstimate(flops=6 * rows * width * 16 * width, bytes_accessed=4 * rows * width, transcendentals=0),
        name="newton_schulz",
    )(iterate)


def solution(mesh):
    return jax.shard_map(
        shards, mesh=mesh, in_specs=(P("fsdp", "tensor"),), out_specs=P("fsdp", "tensor"), check_vma=False
    )
```

time: 209 us -> 176 us (0.84)
  Pallas kernels: 204 us -> 171 us
    pallas_call x1, Pallas kernels: 204 us -> 171 us  [shards(): pl.pallas_call(kernel, out_shape=jax.ShapeDtypeStruct((rows, width), BF16...]
where the time goes in v3:
time: 176 us
  Pallas kernels  171 us (97%)
  local copies, waits for them, and re-layouts  4.82 us (3%)
    pallas_call x1, Pallas kernels, shards(): pl.pallas_call(kernel, out_shape=jax.ShapeDtypeStruct((rows, width), BF16...  171 us

profile of v3, /device:TPU:1, one launch (start us, length us, event | category | flops | bytes accessed | tf_op | source)
XLA Modules:
  0.0 176.3 jit_solution(1647902966462178675)
XLA Ops:
  0.0 2.4 %copy.2.x_ref = bf16[1600,320]{1,0:T(8,128)(2,1)} copy(bf16[1600,320]{0,1:T(8,128)(2,1)} %param.1) | data formatting | bytes 2048000 | tf_op args[0]
  2.4 171.4 %newton_schulz.1 = bf16[1600,320]{1,0:T(8,128)(2,1)} custom-call(bf16[1600,320]{1,0:T(8,128)(2,1)} %copy.2.x_ref), custom_call_target="tpu_custom_call" | custom-call | flops 15728640000 | bytes 2048000 | tf_op jit(solution)/shard_map/newton_schulz/pallas_call | solution.py:316
  173.9 2.4 %copy.3 = bf16[1600,320]{0,1:T(8,128)(2,1)} copy(bf16[1600,320]{1,0:T(8,128)(2,1)} %newton_schulz.1) | data formatting | bytes 2048000 | tf_op jit(solution)/shard_map/newton_schulz/pallas_call | solution.py:316

commit v4 on v1

v4 whole, which is shorter than its diff:
```python
import functools

import jax
import jax.numpy as jnp
from jax import lax
from jax.experimental import pallas as pl
from jax.experimental.pallas import tpu as pltpu
from jax.sharding import PartitionSpec as P

MESH = pl.DeviceIdType.MESH
BF16, F32 = jnp.bfloat16, jnp.float32
ROWS = 12800
FACTOR = 0.2 * ROWS**0.5
A, B, C = 3.4445, -4.775, 2.0315
GP = 4


class Where:
    def __init__(self):
        f, t = lax.axis_index("fsdp"), lax.axis_index("tensor")
        self.zh, self.x = f // 4, f % 4
        self.y, self.zl, self.c = t // 4, (t // 2) % 2, t % 2

    def device(self, dx=0, dzh=0, dy=0, dzl=0, dc=0):
        x, y = (self.x + dx) % 4, (self.y + dy) % 4
        zh, zl, c = (self.zh + dzh) % 2, (self.zl + dzl) % 2, (self.c + dc) % 2
        return (zh * 4 + x, y * 4 + zl * 2 + c)

    def tplace(self, d, dz):
        return (self.y + d) % 4, (self.zl + dz) % 2

    def fplace(self, d, dz):
        return (self.x + d) % 4, (self.zh + dz) % 2


OWN, MINUS, PLUS, OTHER = (0, 0), (-1, 0), (1, 0), (0, 1)
FIRST = {"az": (OWN, (0, 1), None), "ap": (OWN, (1, 0), None), "am": (OWN, (-1, 0), None)}
TWICE = (
    FIRST | {
        "bm": (PLUS, (-1, 0), None), "bz": (PLUS, (0, 1), None), "bp": (OTHER, (1, 0), None),
        "cp": ((-1, 1), (1, 0), 0), "cm": ((1, 1), (-1, 0), 1),
    },
    {"am": ("bm", "bz"), "az": ("bp",), "bp": ("cp",), "bz": ("cm",)},
    [("az",), ("am",), ("ap",), ("bp",), ("bz",), ("bm",), ("cp", "cm")],
)
ONCE = (
    FIRST | {
        "bp": (OTHER, (1, 0), None), "bm": (OTHER, (-1, 0), None), "cp": (MINUS, (1, 0), 0), "cm": (PLUS, (-1, 0), 1),
        "dp": ((-1, 1), (1, 0), 0), "dm": ((1, 1), (-1, 0), 1),
    },
    {"az": ("bp", "bm"), "ap": ("cp",), "am": ("cm",), "bp": ("dp",), "bm": ("dm",)},
    [("az",), ("ap",), ("am",), ("bp",), ("bm",), ("cp", "cm"), ("dp", "dm")],
)
DIRECT = (
    FIRST | {
        "a2": (OWN, (2, 0), None),
        "bp": (OTHER, (1, 0), None), "bm": (OTHER, (-1, 0), None), "b2": (OTHER, (2, 0), None),
    },
    {"az": ("bp", "bm", "b2")},
    [("az",), ("ap",), ("am",), ("a2",), ("bp",), ("bm",), ("b2",)],
)


TASKS = (
    ((0, 0), (0, 0), 0, (0, 0)),
    ((0, 1), (0, 0), 0, (0, 1)),
    ((1, 0), (0, 0), 0, (1, 0)),
    ((0, 1), (1, 0), 1, (-1, 1)),
    ((-1, 0), (0, 0), 0, (-1, 0)),
    ((0, 1), (-1, 0), -1, (1, 1)),
    ((1, 0), (-1, 0), -1, (2, 0)),
    ((1, 1), (-1, 0), -1, (2, 1)),
)
HOPS = (3, 5, 6, 7)


class Gather:
    def __init__(self, way, view, place, device, send, recv):
        self.plan, self.after, self.order = way
        self.view, self.place, self.device, self.send, self.recv = view, place, device, send, recv
        self.names = list(self.plan)
        self.taken = 0

    def copy(self, name, receiving):
        (d, dz), (step, flip), part = self.plan[name]
        if receiving:
            d, dz = d - step, (dz + flip) % 2
        i = self.names.index(name)
        ref = self.view(self.place(d, dz), part)
        return pltpu.make_async_remote_copy(
            src_ref=ref, dst_ref=ref, send_sem=self.send.at[i], recv_sem=self.recv.at[i],
            device_id=self.device(step, flip), device_id_type=MESH,
        )

    def begin(self):
        for name in self.names:
            if name[0] == "a":
                self.copy(name, False).start()

    def take(self):
        names = self.order[self.taken]
        self.taken += 1
        for name in names:
            self.copy(name, True).wait_recv()
            for nxt in self.after.get(name, ()):
                self.copy(nxt, False).start()
        (d, dz), (step, flip), _ = self.plan[names[0]]
        return (d - step + 1) % 4 - 1, (dz + flip) % 2

    def end(self):
        assert self.taken == len(self.order)
        for name in self.names:
            self.copy(name, False).wait_send()


def kernel(
    x_ref, o_ref, xkept, xin, xb, gp, crecv, own, rsst, rsrecv, hopst, hoprecv, rzst, rzrecv, rzown, ga, gc, pc, acc, uo, urecv,
    ts, tr, gs, gr, hs, hr, ps, pr, ks, xs, xr, cs, cr, rss, rsr, hs2, hr2, zs, zr, shs, shr, pss, psr, us, ur,
):
    w = Where()
    c = w.c
    rows, width = x_ref.shape
    half, full, quarter = rows // 2, 2 * width, width // 4
    mate = w.device(dc=1)

    peers = [dict(dc=1), dict(dy=1), dict(dy=-1), dict(dy=2), dict(dzl=1), dict(dx=1), dict(dx=-1), dict(dx=2), dict(dzh=1)]
    barrier = pltpu.get_barrier_semaphore()
    for peer in peers:
        pl.semaphore_signal(barrier, inc=1, device_id=w.device(**peer), device_id_type=MESH)
    pl.semaphore_wait(barrier, len(peers))

    def remote(src, dst, send, recv, device):
        return pltpu.make_async_remote_copy(
            src_ref=src, dst_ref=dst, send_sem=send, recv_sem=recv, device_id=device, device_id_type=MESH
        )

    swap = remote(x_ref.at[pl.ds((1 - c) * half, half), :], xin, xs, xr, mate)
    swap.start()
    keep = pltpu.make_async_copy(x_ref.at[pl.ds(c * half, half), :], xkept, ks)
    keep.start()
    mine = w.y * 2 + w.zl
    keep.wait()
    swap.wait_recv()
    kept, got = xkept[...], xin[...]
    xb[mine] = jnp.concatenate([jnp.where(c == 0, kept, got), jnp.where(c == 0, got, kept)], axis=1)

    def tdevice(step, flip):
        return w.device(dy=step, dzl=flip)

    def fdevice(step, flip):
        return w.device(dx=step, dzh=flip)

    def slot_of(rel):
        y, zl = w.tplace(*rel)
        return y * 2 + zl

    part_rows = (half // 32 + 1) * 16

    def xview(place, part):
        at, size = ((0, half), (0, part_rows), (part_rows, half - part_rows))[0 if part is None else part + 1]
        return xb.at[place[0] * 2 + place[1], pl.ds(at, size), :]

    gx = Gather(TWICE, xview, w.tplace, tdevice, ts, tr)
    gx.begin()
    other_rows = pl.ds((1 - c) * width, width)
    kept_rows = pl.ds(c * width, width)
    kept_quarter = pl.ds(c * width + w.x * quarter, quarter)
    done = []

    def gram(task):
        buf = len(done) % GP
        done.append(task)
        j, k = TASKS[task][:2]
        gp[buf] = lax.dot_general(
            xb[slot_of(j)], xb[slot_of(k)], (((0,), (0,)), ((), ())), preferred_element_type=F32
        )
        core_copy(task).start()

    def core_copy(task):
        buf = done.index(task) % GP
        return remote(gp.at[buf, other_rows, :], crecv.at[task], cs.at[task], cr.at[task], mate)

    def x_copy(task, d):
        to = (w.x + d) % 4
        return remote(
            rsst.at[task, pl.ds(to * quarter, quarter), :], rsrecv.at[d - 1, task],
            rss.at[task, d - 1], rsr.at[d - 1, task], w.device(dx=d),
        )

    def hop_copy(task):
        i = HOPS.index(task)
        return remote(hopst.at[i], hoprecv.at[i], hs2.at[i], hr2.at[i], w.device(dy=TASKS[task][2]))

    def z_copy(i):
        return remote(rzst.at[i], rzrecv.at[i], zs.at[i], zr.at[i], w.device(dzh=1))

    def scatter(task):
        buf = done.index(task) % GP
        core_copy(task).wait_recv()
        core_copy(task).wait_send()
        own[task] = gp[buf, kept_quarter, :] + crecv[task, pl.ds(w.x * quarter, quarter), :]
        rsst[task] = (gp[buf, kept_rows, :] + crecv[task]).astype(BF16)
        for d in (1, 2, 3):
            x_copy(task, d).start()

    def summed(task):
        for d in (1, 2, 3):
            x_copy(task, d).wait_recv()
        total = own[task] + sum(rsrecv[d, task].astype(F32) for d in range(3))
        if task in HOPS:
            hopst[HOPS.index(task)] = total.astype(BF16)
            hop_copy(task).start()
        else:
            placed(task, total)

    def hopped(task):
        hop_copy(task).wait_recv()
        placed(task, hoprecv[HOPS.index(task)].astype(F32))

    def placed(task, total):
        i, dz = TASKS[task][3]
        i = i % 4
        there = (w.zl + dz) % 2 != w.zh

        @pl.when(there)
        def _():
            rzst[i] = total.astype(BF16)
            z_copy(i).start()

        @pl.when(jnp.logical_not(there))
        def _():
            rzown[i] = total

    part = (quarter // 32 + 1) * 16
    parts = ((0, quarter), (0, part), (part, quarter - part))

    def chunk(i, way_f, way_t):
        def cview(place, half_of):
            at, size = parts[0 if half_of is None else half_of + 1]
            return gc.at[(w.y + i) % 4, place[1], pl.ds(c * width + place[0] * quarter + at, size), :]

        def aview(place, half_of):
            at, size = parts[0 if half_of is None else half_of + 1]
            return ga.at[place[0] * 2 + place[1], (place[0] + i) % 4, pl.ds(at, size), :]

        return (
            Gather(way_f, cview, w.fplace, fdevice, gs.at[i], gr.at[i]),
            Gather(way_t, aview, w.tplace, tdevice, hs.at[i], hr.at[i]),
        )

    chunks = {0: chunk(0, ONCE, ONCE), 1: chunk(1, ONCE, ONCE), 3: chunk(3, ONCE, ONCE), 2: chunk(2, DIRECT, DIRECT)}

    def share(i, place, other=False):
        x, zh = place
        core = 1 - c if other else c
        ref = gc.at[(w.y + i) % 4, zh, pl.ds(core * width + x * quarter, quarter), :]
        return remote(ref, ref, shs.at[i, x * 2 + zh], shr.at[i, x * 2 + zh], mate)

    def ready(i):
        z_copy(i).wait_recv()
        block = (rzown[i] + rzrecv[i].astype(F32)).astype(BF16)
        at = (w.y + i) % 4
        ga[mine, at] = block
        gc[at, w.zh, kept_quarter, :] = block
        for g in chunks[i]:
            g.begin()
        share(i, w.fplace(0, 0)).start()

    def take_f(i, count):
        for _ in range(count):
            share(i, w.fplace(*chunks[i][0].take())).start()

    def take_t(i, count):
        for _ in range(count):
            chunks[i][1].take()

    gram(0)
    scatter(0)
    summed(0)
    for _ in range(3):
        gx.take()
    gram(1)
    gram(2)
    scatter(1)
    gram(5)
    scatter(2)
    gram(4)
    scatter(5)
    gram(3)
    scatter(4)
    gram(6)
    scatter(3)
    scatter(6)
    summed(1)
    ready(0)
    summed(2)
    summed(5)
    summed(4)
    for _ in range(3):
        gx.take()
    gram(7)
    scatter(7)
    hopped(5)
    ready(1)
    summed(3)
    take_f(0, 3)
    take_t(0, 3)
    summed(6)
    hopped(3)
    ready(3)
    take_f(0, 2)
    take_t(0, 2)
    take_f(1, 3)
    take_t(1, 3)
    gx.take()
    hopped(6)
    summed(7)
    take_f(0, 2)
    take_t(0, 2)
    take_f(1, 2)
    take_t(1, 2)
    hopped(7)
    ready(2)
    take_f(3, 3)
    take_t(3, 3)
    take_f(1, 2)
    take_t(1, 2)
    take_f(3, 2)
    take_t(3, 2)
    take_f(2, 4)
    take_t(2, 4)
    take_f(3, 2)
    take_t(3, 2)
    take_f(2, 3)
    take_t(2, 3)
    for i in range(4):
        for j in range(8):
            share(i, (j // 2, j % 2), True).wait_recv()

    total = jnp.dot(
        jnp.concatenate([ga[j].reshape(width, full) for j in range(8)], axis=1),
        gc[...].reshape(8 * full, full), preferred_element_type=F32,
    )
    value = (C * total + B * ga[mine].reshape(width, full).astype(F32)).astype(BF16)
    for i in range(4):
        pc[i, w.zh, kept_quarter, :] = value[i * quarter:(i + 1) * quarter]

    def pview(place, half_of):
        which = pl.ds(0, 4) if half_of is None else pl.ds(2 * half_of, 2)
        return pc.at[which, place[1], pl.ds(c * width + place[0] * quarter, quarter), :]

    def share_p(place, other=False):
        x, zh = place
        core = 1 - c if other else c
        ref = pc.at[:, zh, pl.ds(core * width + x * quarter, quarter), :]
        return remote(ref, ref, pss.at[x * 2 + zh], psr.at[x * 2 + zh], mate)

    gpc = Gather(TWICE, pview, w.fplace, fdevice, ps, pr)
    gpc.begin()
    share_p(w.fplace(0, 0)).start()
    tile_rows = half // 5

    def product(zh, first):
        for x in range(4):
            share_p((x, zh), True).wait_recv()

        left = jnp.concatenate([xb[j * 2 + zh] for j in range(4)], axis=1)
        for at in range(0, full, 256):
            cols = pl.ds(at, min(256, full - at))
            right = jnp.concatenate([pc[j, zh, :, cols] for j in range(4)], axis=0)
            start = A * xb[mine, :, cols].astype(F32) if first else acc[:, cols]
            acc[:, cols] = start + jnp.dot(left, right, preferred_element_type=F32)

    for i in range(7):
        if i == 6:
            product(w.zh, True)
        share_p(w.fplace(*gpc.take())).start()
    product(1 - w.zh, False)

    back = remote(uo, urecv, us, ur, mate)

    def split(i, _):
        at = pl.ds(pl.multiple_of(i * tile_rows, tile_rows), tile_rows)
        value = (FACTOR * acc[at, :]).astype(BF16)
        left, right = value[:, :width], value[:, width:]
        first = c == 0
        o_ref[pl.ds(pl.multiple_of(c * half + i * tile_rows, 16), tile_rows), :] = jnp.where(first, left, right)
        uo[at, :] = jnp.where(first, right, left)
        return 0

    lax.fori_loop(0, 5, split, 0)
    back.start()

    swap.wait_send()
    for g in [gx, gpc] + [g for pair in chunks.values() for g in pair]:
        g.end()
    for step in range(8):
        for d in (1, 2, 3):
            x_copy(step, d).wait_send()
    for task in HOPS:
        hop_copy(task).wait_send()
    for i in range(4):
        z_copy(i).wait_send()
    for j in range(8):
        share_p((j // 2, j % 2)).wait_send()
        for i in range(4):
            share(i, (j // 2, j % 2)).wait_send()
    back.wait()
    o_ref[pl.ds((1 - c) * half, half), :] = urecv[...]


def shards(iterate):
    rows, width = iterate.shape
    half, full, quarter = rows // 2, 2 * width, width // 4
    dma = pltpu.SemaphoreType.DMA
    vmem = pltpu.VMEM
    return pl.pallas_call(
        kernel,
        out_shape=jax.ShapeDtypeStruct((rows, width), BF16),
        in_specs=[pl.BlockSpec(memory_space=pl.ANY)],
        out_specs=pl.BlockSpec(memory_space=pltpu.VMEM),
        scratch_shapes=[
            vmem((half, width), BF16),
            vmem((half, width), BF16),
            vmem((8, half, full), BF16),
            vmem((GP, full, full), F32),
            vmem((8, width, full), F32),
            vmem((8, quarter, full), F32),
            vmem((8, width, full), BF16),
            vmem((3, 8, quarter, full), BF16),
            vmem((4, quarter, full), BF16),
            vmem((4, quarter, full), BF16),
            vmem((4, quarter, full), BF16),
            vmem((4, quarter, full), BF16),
            vmem((4, quarter, full), F32),
            vmem((8, 4, quarter, full), BF16),
            vmem((4, 2, full, full), BF16),
            vmem((4, 2, full, full), BF16),
            vmem((half, full), F32),
            vmem((half, width), BF16),
            vmem((half, width), BF16),
            dma((8,)), dma((8,)), dma((4, 9)), dma((4, 9)), dma((4, 9)), dma((4, 9)), dma((8,)), dma((8,)),
            dma, dma, dma, dma((8,)), dma((8,)), dma((8, 3)), dma((3, 8)), dma((4,)), dma((4,)), dma((4,)), dma((4,)),
            dma((4, 8)), dma((4, 8)), dma((8,)), dma((8,)), dma, dma,
        ],
        compiler_params=pltpu.CompilerParams(
            collective_id=0, has_side_effects=True, vmem_limit_bytes=60 * 2**20
        ),
        cost_estimate=pl.CostEstimate(flops=6 * rows * width * 16 * width, bytes_accessed=4 * rows * width, transcendentals=0),
        name="newton_schulz",
    )(iterate)


def solution(mesh):
    return jax.shard_map(
        shards, mesh=mesh, in_specs=(P("fsdp", "tensor"),), out_specs=P("fsdp", "tensor"), check_vma=False
    )
```

time: 404 us -> 159 us (0.39)
  waiting for transfers between devices: 354 us -> 0 us
  Pallas kernels: 0 us -> 154 us
  matrix products: 30.7 us -> 0 us
  between operations: 13.2 us -> 0.01 us
    all_gather x4 -> x0, waiting for transfers between devices: 270 us -> none  [the longest x1 98.3 us: shards(): gathered = lax.all_gather(iterate, 'tensor', axis=1, tiled=True)]
    pallas_call x0 -> x1, Pallas kernels: none -> 154 us  [shards(): pl.pallas_call(kernel, out_shape=jax.ShapeDtypeStruct((rows, width), BF16...]
    unnamed x6 -> x0, waiting for transfers between devices: 84.3 us -> none
    dot_general x3 -> x0, matrix products: 30.7 us -> none  [the longest x1 13.5 us: shards(): product = jnp.dot(gathered, panel, preferred_element_type=jnp.float32)]
  transfers between devices with their start and end apart: 5 -> 0, of which waited for: 5 -> 0; matrix products, arithmetic and copies ran while one was open for 0% -> 0% of each run, Pallas kernels for 0% -> 0%
where the time goes in v4:
time: 159 us; the launch traced here: 158 us
  Pallas kernels  154 us (97%)
  local copies, waits for them, and re-layouts  4.82 us (3%)
    pallas_call x1, Pallas kernels, shards(): pl.pallas_call(kernel, out_shape=jax.ShapeDtypeStruct((rows, width), BF16...  154 us

profile of v4, /device:TPU:1, one launch (start us, length us, event | category | flops | bytes accessed | tf_op | source)
XLA Modules:
  0.0 158.5 jit_solution(18292848597361597581)
XLA Ops:
  0.0 2.4 %copy.2.x_ref = bf16[1600,320]{1,0:T(8,128)(2,1)} copy(bf16[1600,320]{0,1:T(8,128)(2,1)} %param.1) | data formatting | bytes 2048000 | tf_op args[0]
  2.4 153.6 %newton_schulz.1 = bf16[1600,320]{1,0:T(8,128)(2,1)} custom-call(bf16[1600,320]{1,0:T(8,128)(2,1)} %copy.2.x_ref), custom_call_target="tpu_custom_call" | custom-call | flops 15728640000 | bytes 2048000 | tf_op jit(solution)/shard_map/newton_schulz/pallas_call | solution.py:417
  156.0 2.4 %copy.3 = bf16[1600,320]{0,1:T(8,128)(2,1)} copy(bf16[1600,320]{1,0:T(8,128)(2,1)} %newton_schulz.1) | data formatting | bytes 2048000 | tf_op jit(solution)/shard_map/newton_schulz/pallas_call | solution.py:417

commit v5 on v4

--- a/solution.py
+++ b/solution.py
@@ -51,6 +51,14 @@
     {"az": ("bp", "bm"), "ap": ("cp",), "am": ("cm",), "bp": ("dp",), "bm": ("dm",)},
     [("az",), ("ap",), ("am",), ("bp",), ("bm",), ("cp", "cm"), ("dp", "dm")],
 )
+HELD = (
+    FIRST | {
+        "bm": (OTHER, (-1, 0), 0), "bz": (PLUS, (0, 1), 1), "bp": (OTHER, (1, 0), None), "cp": (MINUS, (1, 0), 0),
+        "cm": (PLUS, (-1, 0), 1), "dp": ((-1, 1), (1, 0), 0), "dm": ((1, 1), (-1, 0), 1),
+    },
+    {"az": ("bm", "bp"), "am": ("bz",)},
+    [("az",), ("am",), ("ap",), ("bm", "bz"), ("bp",), ("cp", "cm"), ("dp", "dm")],
+)
 DIRECT = (
     FIRST | {
         "a2": (OWN, (2, 0), None),
@@ -114,7 +122,7 @@
 
 
 def kernel(
-    x_ref, o_ref, xkept, xin, xb, gp, crecv, own, rsst, rsrecv, hopst, hoprecv, rzst, rzrecv, rzown, ga, gc, pc, acc, uo, urecv,
+    x_ref, o_ref, xkept, xin, xb, gp, crecv, own, rsst, rlrecv, rsrecv, hopst, hoprecv, rzst, rzrecv, rzown, ga, gc, pc, acc, uo, urecv,
     ts, tr, gs, gr, hs, hr, ps, pr, ks, xs, xr, cs, cr, rss, rsr, hs2, hr2, zs, zr, shs, shr, pss, psr, us, ur,
 ):
     w = Where()
@@ -160,7 +168,7 @@
         at, size = ((0, half), (0, part_rows), (part_rows, half - part_rows))[0 if part is None else part + 1]
         return xb.at[place[0] * 2 + place[1], pl.ds(at, size), :]
 
-    gx = Gather(TWICE, xview, w.tplace, tdevice, ts, tr)
+    gx = Gather(HELD, xview, w.tplace, tdevice, ts, tr)
     gx.begin()
     other_rows = pl.ds((1 - c) * width, width)
     kept_rows = pl.ds(c * width, width)
@@ -180,11 +188,19 @@
         buf = done.index(task) % GP
         return remote(gp.at[buf, other_rows, :], crecv.at[task], cs.at[task], cr.at[task], mate)
 
-    def x_copy(task, d):
-        to = (w.x + d) % 4
+    cut = (quarter // 32 + 1) * 16
+
+    def relay_copy(task, way):
+        at, size = ((0, cut), (cut, quarter - cut))[way]
         return remote(
-            rsst.at[task, pl.ds(to * quarter, quarter), :], rsrecv.at[d - 1, task],
-            rss.at[task, d - 1], rsr.at[d - 1, task], w.device(dx=d),
+            rsst.at[task, pl.ds((w.x + 2) % 4 * quarter + at, size), :], rlrecv.at[task, pl.ds(at, size), :],
+            rss.at[task, way], rsr.at[task, way], w.device(dx=1 - 2 * way),
+        )
+
+    def x_copy(task, way):
+        return remote(
+            rsst.at[task, pl.ds((w.x + 1 - 2 * way) % 4 * quarter, quarter), :], rsrecv.at[way, task],
+            rss.at[task, 2 + way], rsr.at[task, 2 + way], w.device(dx=1 - 2 * way),
         )
 
     def hop_copy(task):
@@ -200,13 +216,22 @@
         core_copy(task).wait_send()
         own[task] = gp[buf, kept_quarter, :] + crecv[task, pl.ds(w.x * quarter, quarter), :]
         rsst[task] = (gp[buf, kept_rows, :] + crecv[task]).astype(BF16)
-        for d in (1, 2, 3):
-            x_copy(task, d).start()
+        for way in (0, 1):
+            relay_copy(task, way).start()
+
+    def relayed(task):
+        for way, (at, size) in enumerate(((0, cut), (cut, quarter - cut))):
+            relay_copy(task, way).wait_recv()
+            rows = pl.ds((w.x + 1 - 2 * way) % 4 * quarter + at, size)
+            rsst[task, rows, :] = (
+                rsst[task, rows, :].astype(F32) + rlrecv[task, pl.ds(at, size), :].astype(F32)
+            ).astype(BF16)
+            x_copy(task, way).start()
 
     def summed(task):
-        for d in (1, 2, 3):
-            x_copy(task, d).wait_recv()
-        total = own[task] + sum(rsrecv[d, task].astype(F32) for d in range(3))
+        for way in (0, 1):
+            x_copy(task, way).wait_recv()
+        total = own[task] + rsrecv[0, task].astype(F32) + rsrecv[1, task].astype(F32)
         if task in HOPS:
             hopst[HOPS.index(task)] = total.astype(BF16)
             hop_copy(task).start()
@@ -276,6 +301,7 @@
 
     gram(0)
     scatter(0)
+    relayed(0)
     summed(0)
     for _ in range(3):
         gx.take()
@@ -285,127 +311,166 @@
     gram(5)
     scatter(2)
     gram(4)
+    relayed(1)
     scatter(5)
     gram(3)
+    relayed(2)
     scatter(4)
     gram(6)
+    relayed(5)
     scatter(3)
+    relayed(4)
     scatter(6)
+    relayed(3)
+    for _ in range(1):
+        gx.take()
+    gram(7)
     summed(1)
     ready(0)
+    relayed(6)
+    scatter(7)
     summed(2)
     summed(5)
+    take_f(0, 1)
+    take_t(0, 1)
     summed(4)
-    for _ in range(3):
-        gx.take()
-    gram(7)
-    scatter(7)
+    relayed(7)
     hopped(5)
     ready(1)
+    take_f(0, 2)
+    take_t(0, 2)
     summed(3)
-    take_f(0, 3)
-    take_t(0, 3)
     summed(6)
     hopped(3)
+    take_f(1, 1)
+    take_t(1, 1)
     ready(3)
-    take_f(0, 2)
-    take_t(0, 2)
-    take_f(1, 3)
-    take_t(1, 3)
-    gx.take()
+    summed(7)
     hopped(6)
-    summed(7)
     take_f(0, 2)
     take_t(0, 2)
     take_f(1, 2)
     take_t(1, 2)
+    take_f(3, 1)
+    take_t(3, 1)
     hopped(7)
     ready(2)
-    take_f(3, 3)
-    take_t(3, 3)
+    take_f(0, 2)
+    take_t(0, 2)
     take_f(1, 2)
     take_t(1, 2)
     take_f(3, 2)
     take_t(3, 2)
-    take_f(2, 4)
-    take_t(2, 4)
+    take_f(2, 1)
+    take_t(2, 1)
+    take_f(2, 2)
+    take_t(2, 2)
+    take_f(1, 2)
+    take_t(1, 2)
     take_f(3, 2)
     take_t(3, 2)
-    take_f(2, 3)
-    take_t(2, 3)
+    take_f(2, 2)
+    take_t(2, 2)
+    take_f(3, 2)
+    take_t(3, 2)
+    take_f(2, 2)
+    take_t(2, 2)
+    for _ in range(1):
+        gx.take()
+    for name in ("cp", "cm", "dp", "dm"):
+        gx.copy(name, False).start()
     for i in range(4):
         for j in range(8):
             share(i, (j // 2, j % 2), True).wait_recv()
 
-    total = jnp.dot(
-        jnp.concatenate([ga[j].reshape(width, full) for j in range(8)], axis=1),
-        gc[...].reshape(8 * full, full), preferred_element_type=F32,
-    )
-    value = (C * total + B * ga[mine].reshape(width, full).astype(F32)).astype(BF16)
-    for i in range(4):
-        pc[i, w.zh, kept_quarter, :] = value[i * quarter:(i + 1) * quarter]
-
-    def pview(place, half_of):
-        which = pl.ds(0, 4) if half_of is None else pl.ds(2 * half_of, 2)
-        return pc.at[which, place[1], pl.ds(c * width + place[0] * quarter, quarter), :]
-
-    def share_p(place, other=False):
+    columns = [pl.ds(at, min(384, full - at)) for at in range(0, full, 384)]
+
+    def pview(cols):
+        def view(place, half_of):
+            which = pl.ds(0, 4) if half_of is None else pl.ds(2 * half_of, 2)
+            return pc.at[which, place[1], pl.ds(c * width + place[0] * quarter, quarter), cols]
+
+        return view
+
+    def share_p(n, place, other=False):
         x, zh = place
         core = 1 - c if other else c
-        ref = pc.at[:, zh, pl.ds(core * width + x * quarter, quarter), :]
-        return remote(ref, ref, pss.at[x * 2 + zh], psr.at[x * 2 + zh], mate)
-
-    gpc = Gather(TWICE, pview, w.fplace, fdevice, ps, pr)
-    gpc.begin()
-    share_p(w.fplace(0, 0)).start()
-    tile_rows = half // 5
-
-    def product(zh, first):
+        ref = pc.at[:, zh, pl.ds(core * width + x * quarter, quarter), columns[n]]
+        return remote(ref, ref, pss.at[n, x * 2 + zh], psr.at[n, x * 2 + zh], mate)
+
+    gps = [Gather(TWICE, pview(cols), w.fplace, fdevice, ps.at[n], pr.at[n]) for n, cols in enumerate(columns)]
+    for n, cols in enumerate(columns):
+        total = jnp.dot(
+            jnp.concatenate([ga[j].reshape(width, full) for j in range(8)], axis=1),
+            jnp.concatenate([gc[j // 2, j % 2, :, cols] for j in range(8)], axis=0),
+            preferred_element_type=F32,
+        )
+        value = (C * total + B * ga[mine, :, :, cols].reshape(width, cols.size).astype(F32)).astype(BF16)
+        for i in range(4):
+            pc[i, w.zh, kept_quarter, cols] = value[i * quarter:(i + 1) * quarter]
+        gps[n].begin()
+        share_p(n, w.fplace(0, 0)).start()
+
+    def take_p(n):
+        share_p(n, w.fplace(*gps[n].take())).start()
+
+    def arrived(n, zh):
         for x in range(4):
-            share_p((x, zh), True).wait_recv()
-
-        left = jnp.concatenate([xb[j * 2 + zh] for j in range(4)], axis=1)
-        for at in range(0, full, 256):
-            cols = pl.ds(at, min(256, full - at))
-            right = jnp.concatenate([pc[j, zh, :, cols] for j in range(4)], axis=0)
-            start = A * xb[mine, :, cols].astype(F32) if first else acc[:, cols]
-            acc[:, cols] = start + jnp.dot(left, right, preferred_element_type=F32)
-
-    for i in range(7):
-        if i == 6:
-            product(w.zh, True)
-        share_p(w.fplace(*gpc.take())).start()
-    product(1 - w.zh, False)
-
-    back = remote(uo, urecv, us, ur, mate)
-
-    def split(i, _):
-        at = pl.ds(pl.multiple_of(i * tile_rows, tile_rows), tile_rows)
-        value = (FACTOR * acc[at, :]).astype(BF16)
+            share_p(n, (x, zh), True).wait_recv()
+
+    def product(n, zh, first, rows=pl.ds(0, half)):
+        cols = columns[n]
+        left = jnp.concatenate([xb[j * 2 + zh, rows, :] for j in range(4)], axis=1)
+        right = jnp.concatenate([pc[j, zh, :, cols] for j in range(4)], axis=0)
+        start = A * xb[mine, rows, cols].astype(F32) if first else acc[rows, cols]
+        acc[rows, cols] = start + jnp.dot(left, right, preferred_element_type=F32)
+
+    def back(part):
+        rows = pl.ds(part * (half // 2), half // 2)
+        return remote(uo.at[rows, :], urecv.at[rows, :], us.at[part], ur.at[part], mate)
+
+    for _ in range(6):
+        take_p(0)
+        take_p(1)
+    gx.take()
+    gx.take()
+    arrived(0, w.zh)
+    product(0, w.zh, True)
+    take_p(0)
+    arrived(1, w.zh)
+    product(1, w.zh, True)
+    take_p(1)
+    arrived(0, 1 - w.zh)
+    product(0, 1 - w.zh, False)
+    arrived(1, 1 - w.zh)
+    for part in (0, 1):
+        rows = pl.ds(part * (half // 2), half // 2)
+        product(1, 1 - w.zh, False, rows)
+        value = (FACTOR * acc[rows, :]).astype(BF16)
         left, right = value[:, :width], value[:, width:]
         first = c == 0
-        o_ref[pl.ds(pl.multiple_of(c * half + i * tile_rows, 16), tile_rows), :] = jnp.where(first, left, right)
-        uo[at, :] = jnp.where(first, right, left)
-        return 0
-
-    lax.fori_loop(0, 5, split, 0)
-    back.start()
+        uo[rows, :] = jnp.where(first, right, left)
+        back(part).start()
+        o_ref[pl.ds(pl.multiple_of(c * half + part * (half // 2), 16), half // 2), :] = jnp.where(first, left, right)
 
     swap.wait_send()
-    for g in [gx, gpc] + [g for pair in chunks.values() for g in pair]:
+    for g in [gx] + gps + [g for pair in chunks.values() for g in pair]:
         g.end()
     for step in range(8):
-        for d in (1, 2, 3):
-            x_copy(step, d).wait_send()
+        for way in (0, 1):
+            relay_copy(step, way).wait_send()
+            x_copy(step, way).wait_send()
     for task in HOPS:
         hop_copy(task).wait_send()
     for i in range(4):
         z_copy(i).wait_send()
     for j in range(8):
-        share_p((j // 2, j % 2)).wait_send()
+        for n in (0, 1):
+            share_p(n, (j // 2, j % 2)).wait_send()
         for i in range(4):
             share(i, (j // 2, j % 2)).wait_send()
-    back.wait()
+    for part in (0, 1):
+        back(part).wait()
     o_ref[pl.ds((1 - c) * half, half), :] = urecv[...]
 
 
@@ -427,7 +492,8 @@
             vmem((8, width, full), F32),
             vmem((8, quarter, full), F32),
             vmem((8, width, full), BF16),
-            vmem((3, 8, quarter, full), BF16),
+            vmem((8, quarter, full), BF16),
+            vmem((2, 8, quarter, full), BF16),
             vmem((4, quarter, full), BF16),
             vmem((4, quarter, full), BF16),
             vmem((4, quarter, full), BF16),
@@ -439,9 +505,9 @@
             vmem((half, full), F32),
             vmem((half, width), BF16),
             vmem((half, width), BF16),
-            dma((8,)), dma((8,)), dma((4, 9)), dma((4, 9)), dma((4, 9)), dma((4, 9)), dma((8,)), dma((8,)),
-            dma, dma, dma, dma((8,)), dma((8,)), dma((8, 3)), dma((3, 8)), dma((4,)), dma((4,)), dma((4,)), dma((4,)),
-            dma((4, 8)), dma((4, 8)), dma((8,)), dma((8,)), dma, dma,
+            dma((10,)), dma((10,)), dma((4, 9)), dma((4, 9)), dma((4, 9)), dma((4, 9)), dma((2, 8)), dma((2, 8)),
+            dma, dma, dma, dma((8,)), dma((8,)), dma((8, 4)), dma((8, 4)), dma((4,)), dma((4,)), dma((4,)), dma((4,)),
+            dma((4, 8)), dma((4, 8)), dma((2, 8)), dma((2, 8)), dma((2,)), dma((2,)),
         ],
         compiler_params=pltpu.CompilerParams(
             collective_id=0, has_side_effects=True, vmem_limit_bytes=60 * 2**20

time: 159 us -> 151 us (0.950); the launches traced: 158 us -> 149 us
  Pallas kernels: 154 us -> 144 us
    pallas_call x1, Pallas kernels: 154 us -> 144 us  [shards(): pl.pallas_call(kernel, out_shape=jax.ShapeDtypeStruct((rows, width), BF16...]
where the time goes in v5:
time: 151 us; the launch traced here: 149 us
  Pallas kernels  144 us (95%)
  local copies, waits for them, and re-layouts  4.82 us (3%)
    pallas_call x1, Pallas kernels, shards(): pl.pallas_call(kernel, out_shape=jax.ShapeDtypeStruct((rows, width), BF16...  144 us

profile of v5, /device:TPU:1, one launch (start us, length us, event | category | flops | bytes accessed | tf_op | source)
XLA Modules:
  0.0 148.7 jit_solution(8811149936667792561)
XLA Ops:
  0.0 2.4 %copy.2.x_ref = bf16[1600,320]{1,0:T(8,128)(2,1)} copy(bf16[1600,320]{0,1:T(8,128)(2,1)} %param.1) | data formatting | bytes 2048000 | tf_op args[0]
  2.4 143.9 %newton_schulz.1 = bf16[1600,320]{1,0:T(8,128)(2,1)} custom-call(bf16[1600,320]{1,0:T(8,128)(2,1)} %copy.2.x_ref), custom_call_target="tpu_custom_call" | custom-call | flops 15728640000 | bytes 2048000 | tf_op jit(solution)/shard_map/newton_schulz/pallas_call | solution.py:482
  146.3 2.4 %copy.3 = bf16[1600,320]{0,1:T(8,128)(2,1)} copy(bf16[1600,320]{1,0:T(8,128)(2,1)} %newton_schulz.1) | data formatting | bytes 2048000 | tf_op jit(solution)/shard_map/newton_schulz/pallas_call | solution.py:482

commit v6 on v5

--- a/solution.py
+++ b/solution.py
@@ -80,6 +80,8 @@
     ((1, 1), (-1, 0), -1, (2, 1)),
 )
 HOPS = (3, 5, 6, 7)
+ORDER = (0, 1, 3, 2)
+STRAIGHT = (0, 1, 2, 3, 4, 5, 6, 7)
 
 
 class Gather:
@@ -131,7 +133,8 @@
     half, full, quarter = rows // 2, 2 * width, width // 4
     mate = w.device(dc=1)
 
-    peers = [dict(dc=1), dict(dy=1), dict(dy=-1), dict(dy=2), dict(dzl=1), dict(dx=1), dict(dx=-1), dict(dx=2), dict(dzh=1)]
+    peers = [dict(dc=1), dict(dy=1), dict(dy=-1), dict(dy=2), dict(dzl=1), dict(dx=1), dict(dx=-1), dict(dx=2), dict(dzh=1),
+             dict(dy=1, dzh=1), dict(dy=-1, dzh=1)]
     barrier = pltpu.get_barrier_semaphore()
     for peer in peers:
         pl.semaphore_signal(barrier, inc=1, device_id=w.device(**peer), device_id_type=MESH)
@@ -190,11 +193,21 @@
 
     cut = (quarter // 32 + 1) * 16
 
+    def cuts(task):
+        first = cut if task % 2 else quarter - cut
+        return (0, first), (first, quarter - first)
+
     def relay_copy(task, way):
-        at, size = ((0, cut), (cut, quarter - cut))[way]
+        at, size = cuts(task)[way]
         return remote(
             rsst.at[task, pl.ds((w.x + 2) % 4 * quarter + at, size), :], rlrecv.at[task, pl.ds(at, size), :],
             rss.at[task, way], rsr.at[task, way], w.device(dx=1 - 2 * way),
+        )
+
+    def opposite_copy(task):
+        return remote(
+            rsst.at[task, pl.ds((w.x + 2) % 4 * quarter, quarter), :], rlrecv.at[task],
+            rss.at[task, 0], rsr.at[task, 0], w.device(dx=2),
         )
 
     def x_copy(task, way):
@@ -207,8 +220,11 @@
         i = HOPS.index(task)
         return remote(hopst.at[i], hoprecv.at[i], hs2.at[i], hr2.at[i], w.device(dy=TASKS[task][2]))
 
-    def z_copy(i):
-        return remote(rzst.at[i], rzrecv.at[i], zs.at[i], zr.at[i], w.device(dzh=1))
+    def z_copy(i, hop=0):
+        return remote(rzst.at[i], rzrecv.at[i], zs.at[i], zr.at[i], w.device(dy=hop, dzh=1))
+
+    def leaves(task):
+        return (w.zl + TASKS[task][3][1]) % 2 != w.zh
 
     def scatter(task):
         buf = done.index(task) % GP
@@ -216,11 +232,18 @@
         core_copy(task).wait_send()
         own[task] = gp[buf, kept_quarter, :] + crecv[task, pl.ds(w.x * quarter, quarter), :]
         rsst[task] = (gp[buf, kept_rows, :] + crecv[task]).astype(BF16)
-        for way in (0, 1):
-            relay_copy(task, way).start()
+        if task in STRAIGHT:
+            opposite_copy(task).start()
+            for way in (0, 1):
+                x_copy(task, way).start()
+        else:
+            for way in (0, 1):
+                relay_copy(task, way).start()
 
     def relayed(task):
-        for way, (at, size) in enumerate(((0, cut), (cut, quarter - cut))):
+        if task in STRAIGHT:
+            return
+        for way, (at, size) in enumerate(cuts(task)):
             relay_copy(task, way).wait_recv()
             rows = pl.ds((w.x + 1 - 2 * way) % 4 * quarter + at, size)
             rsst[task, rows, :] = (
@@ -232,72 +255,73 @@
         for way in (0, 1):
             x_copy(task, way).wait_recv()
         total = own[task] + rsrecv[0, task].astype(F32) + rsrecv[1, task].astype(F32)
-        if task in HOPS:
-            hopst[HOPS.index(task)] = total.astype(BF16)
-            hop_copy(task).start()
-        else:
-            placed(task, total)
-
-    def hopped(task):
-        hop_copy(task).wait_recv()
-        placed(task, hoprecv[HOPS.index(task)].astype(F32))
-
-    def placed(task, total):
-        i, dz = TASKS[task][3]
+        if task in STRAIGHT:
+            opposite_copy(task).wait_recv()
+            total += rlrecv[task].astype(F32)
+        hop, (i, _) = TASKS[task][2:]
         i = i % 4
-        there = (w.zl + dz) % 2 != w.zh
-
-        @pl.when(there)
+
+        @pl.when(leaves(task))
         def _():
             rzst[i] = total.astype(BF16)
-            z_copy(i).start()
-
-        @pl.when(jnp.logical_not(there))
+            z_copy(i, hop).start()
+
+        @pl.when(jnp.logical_not(leaves(task)))
         def _():
-            rzown[i] = total
-
-    part = (quarter // 32 + 1) * 16
-    parts = ((0, quarter), (0, part), (part, quarter - part))
-
-    def chunk(i, way_f, way_t):
+            if hop:
+                hopst[HOPS.index(task)] = total.astype(BF16)
+                hop_copy(task).start()
+            else:
+                rzown[i] = total
+
+    def hopped(task):
+        @pl.when(jnp.logical_not(leaves(task)))
+        def _():
+            hop_copy(task).wait_recv()
+            rzown[TASKS[task][3][0] % 4] = hoprecv[HOPS.index(task)].astype(F32)
+
+    def chunk(n, way_f, way_t):
+        def which(half_of):
+            return pl.ds(2 * n, 2) if half_of is None else pl.ds(2 * n + half_of, 1)
+
         def cview(place, half_of):
-            at, size = parts[0 if half_of is None else half_of + 1]
-            return gc.at[(w.y + i) % 4, place[1], pl.ds(c * width + place[0] * quarter + at, size), :]
+            return gc.at[which(half_of), place[1], pl.ds(c * width + place[0] * quarter, quarter), :]
 
         def aview(place, half_of):
-            at, size = parts[0 if half_of is None else half_of + 1]
-            return ga.at[place[0] * 2 + place[1], (place[0] + i) % 4, pl.ds(at, size), :]
+            return ga.at[place[0] * 2 + place[1], which(half_of)]
 
         return (
-            Gather(way_f, cview, w.fplace, fdevice, gs.at[i], gr.at[i]),
-            Gather(way_t, aview, w.tplace, tdevice, hs.at[i], hr.at[i]),
-        )
-
-    chunks = {0: chunk(0, ONCE, ONCE), 1: chunk(1, ONCE, ONCE), 3: chunk(3, ONCE, ONCE), 2: chunk(2, DIRECT, DIRECT)}
-
-    def share(i, place, other=False):
+            Gather(way_f, cview, w.fplace, fdevice, gs.at[n], gr.at[n]),
+            Gather(way_t, aview, w.tplace, tdevice, hs.at[n], hr.at[n]),
+        )
+
+    chunks = (chunk(0, ONCE, TWICE), chunk(1, ONCE, TWICE))
+
+    def share(n, place, other=False):
         x, zh = place
         core = 1 - c if other else c
-        ref = gc.at[(w.y + i) % 4, zh, pl.ds(core * width + x * quarter, quarter), :]
-        return remote(ref, ref, shs.at[i, x * 2 + zh], shr.at[i, x * 2 + zh], mate)
+        ref = gc.at[pl.ds(2 * n, 2), zh, pl.ds(core * width + x * quarter, quarter), :]
+        return remote(ref, ref, shs.at[n, x * 2 + zh], shr.at[n, x * 2 + zh], mate)
 
     def ready(i):
         z_copy(i).wait_recv()
         block = (rzown[i] + rzrecv[i].astype(F32)).astype(BF16)
-        at = (w.y + i) % 4
+        at = ORDER.index(i)
         ga[mine, at] = block
         gc[at, w.zh, kept_quarter, :] = block
-        for g in chunks[i]:
+
+    def begin(n):
+        for g in chunks[n]:
             g.begin()
-        share(i, w.fplace(0, 0)).start()
-
-    def take_f(i, count):
+        share(n, w.fplace(0, 0)).start()
+
+    def take_f(n, count):
         for _ in range(count):
-            share(i, w.fplace(*chunks[i][0].take())).start()
-
-    def take_t(i, count):
+            share(n, w.fplace(*chunks[n][0].take())).start()
+
+    def take_t(n, count):
         for _ in range(count):
-            chunks[i][1].take()
+            chunks[n][1].take()
 
     gram(0)
     scatter(0)
@@ -311,77 +335,52 @@
     gram(5)
     scatter(2)
     gram(4)
-    relayed(1)
     scatter(5)
     gram(3)
-    relayed(2)
     scatter(4)
     gram(6)
-    relayed(5)
     scatter(3)
-    relayed(4)
     scatter(6)
-    relayed(3)
     for _ in range(1):
         gx.take()
     gram(7)
+    scatter(7)
     summed(1)
-    ready(0)
-    relayed(6)
-    scatter(7)
     summed(2)
     summed(5)
-    take_f(0, 1)
-    take_t(0, 1)
-    summed(4)
-    relayed(7)
+    ready(0)
     hopped(5)
     ready(1)
-    take_f(0, 2)
-    take_t(0, 2)
+    begin(0)
+    summed(4)
     summed(3)
     summed(6)
+    summed(7)
     hopped(3)
-    take_f(1, 1)
-    take_t(1, 1)
     ready(3)
-    summed(7)
     hopped(6)
+    hopped(7)
+    ready(2)
+    begin(1)
+    take_f(0, 3)
+    take_t(0, 3)
+    take_f(1, 3)
+    take_t(1, 3)
     take_f(0, 2)
     take_t(0, 2)
     take_f(1, 2)
     take_t(1, 2)
-    take_f(3, 1)
-    take_t(3, 1)
-    hopped(7)
-    ready(2)
     take_f(0, 2)
     take_t(0, 2)
     take_f(1, 2)
     take_t(1, 2)
-    take_f(3, 2)
-    take_t(3, 2)
-    take_f(2, 1)
-    take_t(2, 1)
-    take_f(2, 2)
-    take_t(2, 2)
-    take_f(1, 2)
-    take_t(1, 2)
-    take_f(3, 2)
-    take_t(3, 2)
-    take_f(2, 2)
-    take_t(2, 2)
-    take_f(3, 2)
-    take_t(3, 2)
-    take_f(2, 2)
-    take_t(2, 2)
     for _ in range(1):
         gx.take()
     for name in ("cp", "cm", "dp", "dm"):
         gx.copy(name, False).start()
-    for i in range(4):
+    for n in range(2):
         for j in range(8):
-            share(i, (j // 2, j % 2), True).wait_recv()
+            share(n, (j // 2, j % 2), True).wait_recv()
 
     columns = [pl.ds(at, min(384, full - at)) for at in range(0, full, 384)]
 
@@ -399,15 +398,20 @@
         return remote(ref, ref, pss.at[n, x * 2 + zh], psr.at[n, x * 2 + zh], mate)
 
     gps = [Gather(TWICE, pview(cols), w.fplace, fdevice, ps.at[n], pr.at[n]) for n, cols in enumerate(columns)]
+    def rows_of(at, zl):
+        slot = (w.y + ORDER[at]) % 4 * 2 + zl
+        return jnp.concatenate([ga[slot, ORDER.index((i - ORDER[at]) % 4)] for i in ORDER], axis=0)
+
+    depth = [(at, zl) for at in range(4) for zl in range(2)]
     for n, cols in enumerate(columns):
         total = jnp.dot(
-            jnp.concatenate([ga[j].reshape(width, full) for j in range(8)], axis=1),
-            jnp.concatenate([gc[j // 2, j % 2, :, cols] for j in range(8)], axis=0),
+            jnp.concatenate([rows_of(at, zl) for at, zl in depth], axis=1),
+            jnp.concatenate([gc[at, zl, :, cols] for at, zl in depth], axis=0),
             preferred_element_type=F32,
         )
         value = (C * total + B * ga[mine, :, :, cols].reshape(width, cols.size).astype(F32)).astype(BF16)
-        for i in range(4):
-            pc[i, w.zh, kept_quarter, cols] = value[i * quarter:(i + 1) * quarter]
+        for at, i in enumerate(ORDER):
+            pc[(w.y + i) % 4, w.zh, kept_quarter, cols] = value[at * quarter:(at + 1) * quarter]
         gps[n].begin()
         share_p(n, w.fplace(0, 0)).start()
 
@@ -454,21 +458,27 @@
         o_ref[pl.ds(pl.multiple_of(c * half + part * (half // 2), 16), half // 2), :] = jnp.where(first, left, right)
 
     swap.wait_send()
-    for g in [gx] + gps + [g for pair in chunks.values() for g in pair]:
+    for g in [gx] + gps + [g for pair in chunks for g in pair]:
         g.end()
     for step in range(8):
+        if step in STRAIGHT:
+            opposite_copy(step).wait_send()
         for way in (0, 1):
-            relay_copy(step, way).wait_send()
+            if step not in STRAIGHT:
+                relay_copy(step, way).wait_send()
             x_copy(step, way).wait_send()
     for task in HOPS:
-        hop_copy(task).wait_send()
+        @pl.when(jnp.logical_not(leaves(task)))
+        def _(task=task):
+            hop_copy(task).wait_send()
+
     for i in range(4):
         z_copy(i).wait_send()
     for j in range(8):
         for n in (0, 1):
             share_p(n, (j // 2, j % 2)).wait_send()
-        for i in range(4):
-            share(i, (j // 2, j % 2)).wait_send()
+        for n in range(2):
+            share(n, (j // 2, j % 2)).wait_send()
     for part in (0, 1):
         back(part).wait()
     o_ref[pl.ds((1 - c) * half, half), :] = urecv[...]

time: 151 us -> 147 us (0.974); the launches traced: 149 us -> 147 us
  Pallas kernels: 144 us -> 142 us
    pallas_call x1, Pallas kernels: 144 us -> 142 us  [shards(): pl.pallas_call(kernel, out_shape=jax.ShapeDtypeStruct((rows, width), BF16...]
where the time goes in v6:
time: 147 us
  Pallas kernels  142 us (97%)
  local copies, waits for them, and re-layouts  4.82 us (3%)
    pallas_call x1, Pallas kernels, shards(): pl.pallas_call(kernel, out_shape=jax.ShapeDtypeStruct((rows, width), BF16...  142 us

profile of v6, /device:TPU:1, one launch (start us, length us, event | category | flops | bytes accessed | tf_op | source)
XLA Modules:
  0.0 146.8 jit_solution(2348302309271230300)
XLA Ops:
  0.0 2.4 %copy.2.x_ref = bf16[1600,320]{1,0:T(8,128)(2,1)} copy(bf16[1600,320]{0,1:T(8,128)(2,1)} %param.1) | data formatting | bytes 2048000 | tf_op args[0]
  2.4 142.0 %newton_schulz.1 = bf16[1600,320]{1,0:T(8,128)(2,1)} custom-call(bf16[1600,320]{1,0:T(8,128)(2,1)} %copy.2.x_ref), custom_call_target="tpu_custom_call" | custom-call | flops 15728640000 | bytes 2048000 | tf_op jit(solution)/shard_map/newton_schulz/pallas_call | solution.py:492
  144.4 2.4 %copy.3 = bf16[1600,320]{0,1:T(8,128)(2,1)} copy(bf16[1600,320]{1,0:T(8,128)(2,1)} %newton_schulz.1) | data formatting | bytes 2048000 | tf_op jit(solution)/shard_map/newton_schulz/pallas_call | solution.py:492

commit v7 on v6

--- a/solution.py
+++ b/solution.py
@@ -81,7 +81,7 @@
 )
 HOPS = (3, 5, 6, 7)
 ORDER = (0, 1, 3, 2)
-STRAIGHT = (0, 1, 2, 3, 4, 5, 6, 7)
+STRAIGHT = (0, 3, 4, 5, 6, 7)
 
 
 class Gather:
@@ -325,7 +325,6 @@
 
     gram(0)
     scatter(0)
-    relayed(0)
     summed(0)
     for _ in range(3):
         gx.take()
@@ -335,8 +334,10 @@
     gram(5)
     scatter(2)
     gram(4)
+    relayed(1)
     scatter(5)
     gram(3)
+    relayed(2)
     scatter(4)
     gram(6)
     scatter(3)
@@ -355,14 +356,14 @@
     summed(4)
     summed(3)
     summed(6)
-    summed(7)
     hopped(3)
     ready(3)
+    summed(7)
+    take_f(0, 3)
     hopped(6)
     hopped(7)
     ready(2)
     begin(1)
-    take_f(0, 3)
     take_t(0, 3)
     take_f(1, 3)
     take_t(1, 3)

time: 147 us -> 146 us (level)
  no operation moved by 1% of the time
where the time goes in v7:
time: 146 us
  Pallas kernels  141 us (97%)
  local copies, waits for them, and re-layouts  4.82 us (3%)
    pallas_call x1, Pallas kernels, shards(): pl.pallas_call(kernel, out_shape=jax.ShapeDtypeStruct((rows, width), BF16...  141 us

profile of v7, /device:TPU:1, one launch (start us, length us, event | category | flops | bytes accessed | tf_op | source)
XLA Modules:
  0.0 146.2 jit_solution(14444064514712932921)
XLA Ops:
  0.0 2.4 %copy.2.x_ref = bf16[1600,320]{1,0:T(8,128)(2,1)} copy(bf16[1600,320]{0,1:T(8,128)(2,1)} %param.1) | data formatting | bytes 2048000 | tf_op args[0]
  2.4 141.4 %newton_schulz.1 = bf16[1600,320]{1,0:T(8,128)(2,1)} custom-call(bf16[1600,320]{1,0:T(8,128)(2,1)} %copy.2.x_ref), custom_call_target="tpu_custom_call" | custom-call | flops 15728640000 | bytes 2048000 | tf_op jit(solution)/shard_map/newton_schulz/pallas_call | solution.py:493
  143.8 2.4 %copy.3 = bf16[1600,320]{0,1:T(8,128)(2,1)} copy(bf16[1600,320]{1,0:T(8,128)(2,1)} %newton_schulz.1) | data formatting | bytes 2048000 | tf_op jit(solution)/shard_map/newton_schulz/pallas_call | solution.py:493

commit v8 on v7

--- a/solution.py
+++ b/solution.py
@@ -52,12 +52,12 @@
     [("az",), ("ap",), ("am",), ("bp",), ("bm",), ("cp", "cm"), ("dp", "dm")],
 )
 HELD = (
-    FIRST | {
+    {name + str(n): (block, way, n) for n in (0, 1) for name, (block, way, _) in FIRST.items()} | {
         "bm": (OTHER, (-1, 0), 0), "bz": (PLUS, (0, 1), 1), "bp": (OTHER, (1, 0), None), "cp": (MINUS, (1, 0), 0),
         "cm": (PLUS, (-1, 0), 1), "dp": ((-1, 1), (1, 0), 0), "dm": ((1, 1), (-1, 0), 1),
     },
-    {"az": ("bm", "bp"), "am": ("bz",)},
-    [("az",), ("am",), ("ap",), ("bm", "bz"), ("bp",), ("cp", "cm"), ("dp", "dm")],
+    {"az0": ("bm",), "az1": ("bp",), "am1": ("bz",)},
+    [("az0", "az1"), ("am0", "am1"), ("ap0", "ap1"), ("bm", "bz"), ("bp",), ("cp", "cm"), ("dp", "dm")],
 )
 DIRECT = (
     FIRST | {
@@ -145,15 +145,23 @@
             src_ref=src, dst_ref=dst, send_sem=send, recv_sem=recv, device_id=device, device_id_type=MESH
         )
 
-    swap = remote(x_ref.at[pl.ds((1 - c) * half, half), :], xin, xs, xr, mate)
-    swap.start()
-    keep = pltpu.make_async_copy(x_ref.at[pl.ds(c * half, half), :], xkept, ks)
-    keep.start()
+    part_rows = (half // 32 + 1) * 16
+    halves = ((0, part_rows), (part_rows, half - part_rows))
+
+    def swap(n):
+        at, size = halves[n]
+        return remote(
+            x_ref.at[pl.ds((1 - c) * half + at, size), :], xin.at[pl.ds(at, size), :], xs.at[n], xr.at[n], mate
+        )
+
+    def keep(n):
+        at, size = halves[n]
+        return pltpu.make_async_copy(x_ref.at[pl.ds(c * half + at, size), :], xkept.at[pl.ds(at, size), :], ks.at[n])
+
+    for n in (0, 1):
+        swap(n).start()
+        keep(n).start()
     mine = w.y * 2 + w.zl
-    keep.wait()
-    swap.wait_recv()
-    kept, got = xkept[...], xin[...]
-    xb[mine] = jnp.concatenate([jnp.where(c == 0, kept, got), jnp.where(c == 0, got, kept)], axis=1)
 
     def tdevice(step, flip):
         return w.device(dy=step, dzl=flip)
@@ -165,14 +173,19 @@
         y, zl = w.tplace(*rel)
         return y * 2 + zl
 
-    part_rows = (half // 32 + 1) * 16
-
     def xview(place, part):
         at, size = ((0, half), (0, part_rows), (part_rows, half - part_rows))[0 if part is None else part + 1]
         return xb.at[place[0] * 2 + place[1], pl.ds(at, size), :]
 
     gx = Gather(HELD, xview, w.tplace, tdevice, ts, tr)
-    gx.begin()
+    for n, (at, size) in enumerate(halves):
+        keep(n).wait()
+        swap(n).wait_recv()
+        rows = pl.ds(at, size)
+        kept, got = xkept[rows, :], xin[rows, :]
+        xb[mine, rows, :] = jnp.concatenate([jnp.where(c == 0, kept, got), jnp.where(c == 0, got, kept)], axis=1)
+        for name in ("az", "am", "ap"):
+            gx.copy(name + str(n), False).start()
     other_rows = pl.ds((1 - c) * width, width)
     kept_rows = pl.ds(c * width, width)
     kept_quarter = pl.ds(c * width + w.x * quarter, quarter)
@@ -458,7 +471,8 @@
         back(part).start()
         o_ref[pl.ds(pl.multiple_of(c * half + part * (half // 2), 16), half // 2), :] = jnp.where(first, left, right)
 
-    swap.wait_send()
+    for n in (0, 1):
+        swap(n).wait_send()
     for g in [gx] + gps + [g for pair in chunks for g in pair]:
         g.end()
     for step in range(8):
@@ -516,8 +530,8 @@
             vmem((half, full), F32),
             vmem((half, width), BF16),
             vmem((half, width), BF16),
-            dma((10,)), dma((10,)), dma((4, 9)), dma((4, 9)), dma((4, 9)), dma((4, 9)), dma((2, 8)), dma((2, 8)),
-            dma, dma, dma, dma((8,)), dma((8,)), dma((8, 4)), dma((8, 4)), dma((4,)), dma((4,)), dma((4,)), dma((4,)),
+            dma((13,)), dma((13,)), dma((4, 9)), dma((4, 9)), dma((4, 9)), dma((4, 9)), dma((2, 8)), dma((2, 8)),
+            dma((2,)), dma((2,)), dma((2,)), dma((8,)), dma((8,)), dma((8, 4)), dma((8, 4)), dma((4,)), dma((4,)), dma((4,)), dma((4,)),
             dma((4, 8)), dma((4, 8)), dma((2, 8)), dma((2, 8)), dma((2,)), dma((2,)),
         ],
         compiler_params=pltpu.CompilerParams(

time: 146 us -> 145 us (level)
    pallas_call x1, Pallas kernels: 141 us -> 140 us  [shards(): pl.pallas_call(kernel, out_shape=jax.ShapeDtypeStruct((rows, width), BF16...]
where the time goes in v8:
time: 145 us
  Pallas kernels  140 us (97%)
  local copies, waits for them, and re-layouts  4.82 us (3%)
    pallas_call x1, Pallas kernels, shards(): pl.pallas_call(kernel, out_shape=jax.ShapeDtypeStruct((rows, width), BF16...  140 us

profile of v8, /device:TPU:1, one launch (start us, length us, event | category | flops | bytes accessed | tf_op | source)
XLA Modules:
  0.0 144.7 jit_solution(9740493654685725995)
XLA Ops:
  0.0 2.4 %copy.2.x_ref = bf16[1600,320]{1,0:T(8,128)(2,1)} copy(bf16[1600,320]{0,1:T(8,128)(2,1)} %param.1) | data formatting | bytes 2048000 | tf_op args[0]
  2.4 139.9 %newton_schulz.1 = bf16[1600,320]{1,0:T(8,128)(2,1)} custom-call(bf16[1600,320]{1,0:T(8,128)(2,1)} %copy.2.x_ref), custom_call_target="tpu_custom_call" | custom-call | flops 15728640000 | bytes 2048000 | tf_op jit(solution)/shard_map/newton_schulz/pallas_call | solution.py:507
  142.3 2.4 %copy.3 = bf16[1600,320]{0,1:T(8,128)(2,1)} copy(bf16[1600,320]{1,0:T(8,128)(2,1)} %newton_schulz.1) | data formatting | bytes 2048000 | tf_op jit(solution)/shard_map/newton_schulz/pallas_call | solution.py:507

commit v9 on v8

--- a/solution.py
+++ b/solution.py
@@ -384,14 +384,14 @@
     take_t(0, 2)
     take_f(1, 2)
     take_t(1, 2)
+    for _ in range(1):
+        gx.take()
+    for name in ("cp", "cm", "dp", "dm"):
+        gx.copy(name, False).start()
     take_f(0, 2)
     take_t(0, 2)
     take_f(1, 2)
     take_t(1, 2)
-    for _ in range(1):
-        gx.take()
-    for name in ("cp", "cm", "dp", "dm"):
-        gx.copy(name, False).start()
     for n in range(2):
         for j in range(8):
             share(n, (j // 2, j % 2), True).wait_recv()

time: 145 us -> 146 us (level)
    pallas_call x1, Pallas kernels: 140 us -> 141 us  [shards(): pl.pallas_call(kernel, out_shape=jax.ShapeDtypeStruct((rows, width), BF16...]
where the time goes in v9:
time: 146 us
  Pallas kernels  141 us (97%)
  local copies, waits for them, and re-layouts  4.82 us (3%)
    pallas_call x1, Pallas kernels, shards(): pl.pallas_call(kernel, out_shape=jax.ShapeDtypeStruct((rows, width), BF16...  141 us

profile of v9, /device:TPU:1, one launch (start us, length us, event | category | flops | bytes accessed | tf_op | source)
XLA Modules:
  0.0 146.3 jit_solution(6039210008237937676)
XLA Ops:
  0.0 2.4 %copy.2.x_ref = bf16[1600,320]{1,0:T(8,128)(2,1)} copy(bf16[1600,320]{0,1:T(8,128)(2,1)} %param.1) | data formatting | bytes 2048000 | tf_op args[0]
  2.4 141.5 %newton_schulz.1 = bf16[1600,320]{1,0:T(8,128)(2,1)} custom-call(bf16[1600,320]{1,0:T(8,128)(2,1)} %copy.2.x_ref), custom_call_target="tpu_custom_call" | custom-call | flops 15728640000 | bytes 2048000 | tf_op jit(solution)/shard_map/newton_schulz/pallas_call | solution.py:507
  143.9 2.4 %copy.3 = bf16[1600,320]{0,1:T(8,128)(2,1)} copy(bf16[1600,320]{1,0:T(8,128)(2,1)} %newton_schulz.1) | data formatting | bytes 2048000 | tf_op jit(solution)/shard_map/newton_schulz/pallas_call | solution.py:507

commit v10 on v8

--- a/solution.py
+++ b/solution.py
@@ -124,7 +124,7 @@
 
 
 def kernel(
-    x_ref, o_ref, xkept, xin, xb, gp, crecv, own, rsst, rlrecv, rsrecv, hopst, hoprecv, rzst, rzrecv, rzown, ga, gc, pc, acc, uo, urecv,
+    x_ref, o_ref, xkept, xin, xb, gp, crecv, csend, own, rsst, rlrecv, rsrecv, hopst, hoprecv, rzst, rzrecv, rzown, ga, gc, pc, acc, uo, urecv,
     ts, tr, gs, gr, hs, hr, ps, pr, ks, xs, xr, cs, cr, rss, rsr, hs2, hr2, zs, zr, shs, shr, pss, psr, us, ur,
 ):
     w = Where()
@@ -198,11 +198,12 @@
         gp[buf] = lax.dot_general(
             xb[slot_of(j)], xb[slot_of(k)], (((0,), (0,)), ((), ())), preferred_element_type=F32
         )
+        csend[buf] = gp[buf, other_rows, :].astype(BF16)
         core_copy(task).start()
 
     def core_copy(task):
         buf = done.index(task) % GP
-        return remote(gp.at[buf, other_rows, :], crecv.at[task], cs.at[task], cr.at[task], mate)
+        return remote(csend.at[buf], crecv.at[task], cs.at[task], cr.at[task], mate)
 
     cut = (quarter // 32 + 1) * 16
 
@@ -243,8 +244,8 @@
         buf = done.index(task) % GP
         core_copy(task).wait_recv()
         core_copy(task).wait_send()
-        own[task] = gp[buf, kept_quarter, :] + crecv[task, pl.ds(w.x * quarter, quarter), :]
-        rsst[task] = (gp[buf, kept_rows, :] + crecv[task]).astype(BF16)
+        own[task] = gp[buf, kept_quarter, :] + crecv[task, pl.ds(w.x * quarter, quarter), :].astype(F32)
+        rsst[task] = (gp[buf, kept_rows, :] + crecv[task].astype(F32)).astype(BF16)
         if task in STRAIGHT:
             opposite_copy(task).start()
             for way in (0, 1):
@@ -514,7 +515,8 @@
             vmem((half, width), BF16),
             vmem((8, half, full), BF16),
             vmem((GP, full, full), F32),
-            vmem((8, width, full), F32),
+            vmem((8, width, full), BF16),
+            vmem((GP, width, full), BF16),
             vmem((8, quarter, full), F32),
             vmem((8, width, full), BF16),
             vmem((8, quarter, full), BF16),

time: 145 us -> 145 us (level)
  no operation moved by 1% of the time
where the time goes in v10:
time: 145 us
  Pallas kernels  140 us (97%)
  local copies, waits for them, and re-layouts  4.82 us (3%)
    pallas_call x1, Pallas kernels, shards(): pl.pallas_call(kernel, out_shape=jax.ShapeDtypeStruct((rows, width), BF16...  140 us

profile of v10, /device:TPU:1, one launch (start us, length us, event | category | flops | bytes accessed | tf_op | source)
XLA Modules:
  0.0 145.0 jit_solution(8147768737420971309)
XLA Ops:
  0.0 2.4 %copy.2.x_ref = bf16[1600,320]{1,0:T(8,128)(2,1)} copy(bf16[1600,320]{0,1:T(8,128)(2,1)} %param.1) | data formatting | bytes 2048000 | tf_op args[0]
  2.4 140.2 %newton_schulz.1 = bf16[1600,320]{1,0:T(8,128)(2,1)} custom-call(bf16[1600,320]{1,0:T(8,128)(2,1)} %copy.2.x_ref), custom_call_target="tpu_custom_call" | custom-call | flops 15728640000 | bytes 2048000 | tf_op jit(solution)/shard_map/newton_schulz/pallas_call | solution.py:508
  142.6 2.4 %copy.3 = bf16[1600,320]{0,1:T(8,128)(2,1)} copy(bf16[1600,320]{1,0:T(8,128)(2,1)} %newton_schulz.1) | data formatting | bytes 2048000 | tf_op jit(solution)/shard_map/newton_schulz/pallas_call | solution.py:508
